TPU v7x, 32 devices: a whole 2x2x4 slice. The times are simulated.
32 devices in a mesh: dp: 8 (over y, x, core), tensor: 4 (over z).
Axes of the slice: x: 2, y: 2, z: 4, core: 2. Of those that a mesh axis runs over, the one named last changes fastest.
Arguments:
- inputs: bfloat16 [32768, 768], P(('dp', 'tensor')), may hold values from -6 to 6
- encoded: bfloat16 [32768, 768], P(('dp', 'tensor')), may hold values from -6 to 6
- cotangent: bfloat16 [32768, 768], P(('dp', 'tensor')), may hold values from -6 to 6
- tgt_seg: int32 [32, 1024], P('dp'), may hold values from 0 to 4, as said below
- src_seg: int32 [32, 1024], P('dp'), may hold values from 0 to 4, as said below
- self_qkv: bfloat16 [3, 768, 768], P(None, None, 'tensor'), may hold values from -0.21875 to 0.21875
- self_out: bfloat16 [768, 768], P('tensor'), may hold values from -1.75 to 1.75
- cross_q: bfloat16 [768, 768], P(None, 'tensor'), may hold values from -0.21875 to 0.21875
- cross_kv: bfloat16 [2, 768, 768], P(None, None, 'tensor'), may hold values from -0.21875 to 0.21875
- cross_out: bfloat16 [768, 768], P('tensor'), may hold values from -1.75 to 1.75
- ffn_up: bfloat16 [768, 3072], P(None, 'tensor'), may hold values from -0.21875 to 0.21875
- ffn_down: bfloat16 [3072, 768], P('tensor'), may hold values from -0.109375 to 0.109375
- gains: float32 [3, 768], replicated, may hold values from 0.5 to 1.5
- shifts: float32 [3, 768], replicated, may hold values from -3 to 3
Outputs:
- layer_out: bfloat16 [32768, 768], P(('dp', 'tensor'))
- grad_inputs: bfloat16 [32768, 768], P(('dp', 'tensor'))
- grad_encoded: bfloat16 [32768, 768], P(('dp', 'tensor'))
- grad_self_qkv: float32 [3, 768, 768], P(None, None, 'tensor')
- grad_self_out: float32 [768, 768], P('tensor')
- grad_cross_q: float32 [768, 768], P(None, 'tensor')
- grad_cross_kv: float32 [2, 768, 768], P(None, None, 'tensor')
- grad_cross_out: float32 [768, 768], P('tensor')
- grad_ffn_up: float32 [768, 3072], P(None, 'tensor')
- grad_ffn_down: float32 [3072, 768], P('tensor')
- grad_gains: float32 [3, 768], replicated
- grad_shifts: float32 [3, 768], replicated
Inputs may be any that keep to these rules, and one draw needn't show every extreme that they name: `tgt_seg`: along each row the ids never fall; every id from 0 to 4 occurs in every row, and 4 marks the 1 to 128 padding positions at the row's end. `src_seg`: along each row the ids never fall; every id from 0 to 4 occurs in every row, and 4 marks the 1 to 128 padding positions at the row's end.
All inputs are finite; a program needn't handle non-finite values.
Results may differ from a plain program's by a relative error of at most 0.028.
Values may be sent and summed in bfloat16 or wider, within the bound.
A program may use at most 256 MiB of HBM per device.

v0:
```python
import functools
import jax, jax.numpy as jnp
from jax import lax
from jax.sharding import PartitionSpec as P
from jax.experimental import pallas as pl
from jax.experimental.pallas import tpu as pltpu

HDIM = 64
LANES = 128
MASKED = -1e30
EPSILON = 1e-5
F32 = jnp.float32
BF16 = jnp.bfloat16
NT = (((1,), (1,)), ((), ()))
TN = (((0,), (0,)), ((), ()))
NN = (((1,), (0,)), ((), ()))


def dot(a, b, dims):
    return lax.dot_general(a, b, dims, preferred_element_type=F32)


def by_head(x):
    first = lax.broadcasted_iota(jnp.int32, x.shape, 1) < HDIM
    zero = jnp.zeros_like(x)
    return jnp.concatenate([jnp.where(first, x, zero), jnp.where(first, zero, x)], axis=0)


def later_keys(bk, bq, offset):
    row = lax.broadcasted_iota(jnp.int32, (bk, bq), 1)
    col = lax.broadcasted_iota(jnp.int32, (bk, bq), 0)
    late = col > row + offset
    return jnp.concatenate([late, late], axis=1)


def stacked(x):
    n = x.shape[1] // 2
    return jnp.concatenate([x[:, :n], x[:, n:]], axis=0)


def attend_kernel(causal, block, per, lo_ref, hi_ref, q_ref, k_ref, v_ref, fq_ref, fk_ref, o_ref, lse_ref, scores, acc):
    n = q_ref.shape[0]
    for i in range(n // block):
        rows = pl.ds(i * block, block)
        fq = fq_ref[rows, :]
        fq = jnp.concatenate([fq, fq], axis=0)
        qs = [
            jnp.concatenate(
                [by_head(q_ref[rows, h * LANES : (h + 1) * LANES] * jnp.asarray(HDIM ** -0.5, BF16)), fq], axis=1
            )
            for h in range(per)
        ]

        def score(j, tops, diagonal=False):
            keys = pl.ds(pl.multiple_of(j * block, block), block)
            fk = fk_ref[keys, :]
            out = []
            for h in range(per):
                k = k_ref[keys, h * LANES : (h + 1) * LANES]
                s = dot(jnp.concatenate([k, fk], axis=1), qs[h], NT)
                if diagonal:
                    s = jnp.where(later_keys(block, block, 0), MASKED, s)
                scores[h, keys, :] = s
                out.append(jnp.maximum(tops[h], jnp.max(s, axis=0, keepdims=True)))
            return tuple(out)

        def mix(j, totals, tops):
            keys = pl.ds(pl.multiple_of(j * block, block), block)
            out = []
            for h in range(per):
                p = jnp.exp(scores[h, keys, :] - tops[h])
                out.append(totals[h] + jnp.sum(p, axis=0, keepdims=True))
                v = by_head(v_ref[keys, h * LANES : (h + 1) * LANES])
                acc[h] += dot(stacked(p.astype(BF16)), v, TN)
            return tuple(out)

        tops = tuple(jnp.full((1, 2 * block), MASKED, F32) for _ in range(per))
        totals = tuple(jnp.zeros((1, 2 * block), F32) for _ in range(per))
        acc[...] = jnp.zeros_like(acc)
        if causal:
            tops = score(i, tops, True)
            tops = lax.fori_loop(lo_ref[i], i, score, tops)
            totals = lax.fori_loop(lo_ref[i], i + 1, functools.partial(mix, tops=tops), totals)
        else:
            tops = lax.fori_loop(lo_ref[i], hi_ref[i], score, tops)
            totals = lax.fori_loop(lo_ref[i], hi_ref[i], functools.partial(mix, tops=tops), totals)
        for h in range(per):
            inverse = 1.0 / totals[h]
            inverse = jnp.concatenate(
                [jnp.broadcast_to(inverse[:, side * block : (side + 1) * block], (HDIM, block)) for side in range(2)], axis=0
            )
            o_ref[rows, h * LANES : (h + 1) * LANES] = (acc[h] * inverse.T).astype(BF16)
            lse_ref[h, i] = tops[h] + jnp.log(totals[h])


def attend_back_kernel(
    causal, block, per, lo_ref, hi_ref, q_ref, k_ref, v_ref, fq_ref, fk_ref, g_ref, o_ref, lse_ref,
    dq_ref, dk_ref, dv_ref, dq_acc, dk_acc, dv_acc, qs, gs, delta,
):
    n = q_ref.shape[0]
    m = k_ref.shape[0]
    pick = lax.broadcasted_iota(jnp.int32, (8, LANES), 1) // HDIM == lax.broadcasted_iota(jnp.int32, (8, LANES), 0)
    pick = pick.astype(BF16)
    dq_acc[...] = jnp.zeros_like(dq_acc)
    for h in range(per):
        lanes = slice(h * LANES, (h + 1) * LANES)
        for i in range(n // block):
            rows = pl.ds(i * block, block)
            fq = fq_ref[rows, :]
            qs[h, i, :, :LANES] = by_head(q_ref[rows, lanes] * jnp.asarray(HDIM ** -0.5, BF16))
            qs[h, i, :, LANES:] = jnp.concatenate([fq, fq], axis=0)
            gs[h, i] = by_head(g_ref[rows, lanes])
            prod = g_ref[rows, lanes].astype(F32) * o_ref[rows, lanes].astype(F32)
            high = prod.astype(BF16)
            rest = (prod - high.astype(F32)).astype(BF16)
            sums = dot(pick, high, NT) + dot(pick, rest, NT)
            delta[h, i] = jnp.concatenate([sums[0:1], sums[1:2]], axis=1)
    for j in range(m // block):
        keys = pl.ds(j * block, block)
        fk = fk_ref[keys, :]
        dk_acc[...] = jnp.zeros_like(dk_acc)
        dv_acc[...] = jnp.zeros_like(dv_acc)

        def step(i, _, diagonal=False):
            rows = pl.ds(pl.multiple_of(i * block, block), block)
            ss, dps, ps, dss = [], [], [], []
            for h in range(per):
                lanes = slice(h * LANES, (h + 1) * LANES)
                ss.append(dot(jnp.concatenate([k_ref[keys, lanes], fk], axis=1), qs[h, i], NT))
                dps.append(dot(v_ref[keys, lanes], gs[h, i], NT))
            for h in range(per):
                s = ss[h]
                if diagonal:
                    s = jnp.where(later_keys(block, block, 0), MASKED, s)
                p = jnp.exp(s - lse_ref[h, i])
                ps.append(p.astype(BF16))
                dss.append((p * (dps[h] - delta[h, i])).astype(BF16))
            adds = []
            for h in range(per):
                lanes = slice(h * LANES, (h + 1) * LANES)
                adds.append((dot(ps[h], gs[h, i], NN), dot(dss[h], qs[h, i, :, :LANES], NN), dot(stacked(dss[h]), by_head(k_ref[keys, lanes]), TN)))
            for h in range(per):
                lanes = slice(h * LANES, (h + 1) * LANES)
                dv_acc[h] += adds[h][0]
                dk_acc[h] += adds[h][1]
                dq_acc[rows, lanes] += adds[h][2]
            return 0

        if causal:
            step(j, 0, True)
            lax.fori_loop(j + 1, hi_ref[j], step, 0)
        else:
            lax.fori_loop(lo_ref[j], hi_ref[j], step, 0)
        for h in range(per):
            dk_ref[keys, h * LANES : (h + 1) * LANES] = dk_acc[h].astype(BF16)
            dv_ref[keys, h * LANES : (h + 1) * LANES] = dv_acc[h].astype(BF16)
    dq_ref[...] = (dq_acc[...] * HDIM ** -0.5).astype(BF16)


def block_range(own, other, block, other_block):
    own = own.reshape(-1, block)
    lo = jnp.sum((other[None, :] < own[:, :1]).astype(jnp.int32), axis=1) // other_block
    hi = jnp.sum((other[None, :] <= own[:, -1:]).astype(jnp.int32), axis=1)
    return lo, (hi + other_block - 1) // other_block


def seg_features(q_ids, k_ids):
    lanes = jnp.arange(LANES, dtype=jnp.int32)[None, :]
    fq = jnp.where((lanes < 5) & (q_ids[:, None] != lanes), MASKED, 0.0).astype(BF16)
    fk = (k_ids[:, None] == lanes).astype(BF16)
    return fq, fk


VMEM_LIMIT = 56 * 2**20
FWD_PER = 6
BWD_PER = 3


def attend(q, k, v, q_ids, k_ids, fq, fk, causal, block=256, per=FWD_PER):
    n, width = q.shape
    m = k.shape[0]
    lo, hi = block_range(q_ids, k_ids, block, block)
    wide = per * LANES
    pairs = width // LANES
    col = lambda rows: pl.BlockSpec((rows, wide), lambda i, *_: (0, i))
    whole = lambda rows: pl.BlockSpec((rows, LANES), lambda i, *_: (0, 0))
    vec = pl.BlockSpec((per, n // block, 1, 2 * block), lambda i, *_: (i, 0, 0, 0))
    return pl.pallas_call(
        functools.partial(attend_kernel, causal, block, per),
        out_shape=(
            jax.ShapeDtypeStruct((n, width), BF16),
            jax.ShapeDtypeStruct((pairs, n // block, 1, 2 * block), F32),
        ),
        grid_spec=pltpu.PrefetchScalarGridSpec(
            num_scalar_prefetch=2,
            grid=(pairs // per,),
            in_specs=[col(n), col(m), col(m), whole(n), whole(m)],
            out_specs=[col(n), vec],
            scratch_shapes=[pltpu.VMEM((per, m, 2 * block), F32), pltpu.VMEM((per, block, LANES), F32)],
        ),
        compiler_params=pltpu.CompilerParams(vmem_limit_bytes=VMEM_LIMIT),
        cost_estimate=pl.CostEstimate(flops=int(8e9), bytes_accessed=int(8e6), transcendentals=int(4e6)),
        name="attend",
    )(lo, hi, q, k, v, fq, fk)


def attend_back(q, k, v, g, out, lse, q_ids, k_ids, fq, fk, causal, block=256, per=BWD_PER):
    n, width = q.shape
    m = k.shape[0]
    lo, hi = block_range(k_ids, q_ids, block, block)
    wide = per * LANES
    pairs = width // LANES
    count = n // block
    col = lambda rows: pl.BlockSpec((rows, wide), lambda i, *_: (0, i))
    whole = lambda rows: pl.BlockSpec((rows, LANES), lambda i, *_: (0, 0))
    vec = pl.BlockSpec((per, count, 1, 2 * block), lambda i, *_: (i, 0, 0, 0))
    return pl.pallas_call(
        functools.partial(attend_back_kernel, causal, block, per),
        out_shape=(
            jax.ShapeDtypeStruct((n, width), BF16),
            jax.ShapeDtypeStruct((m, width), BF16),
            jax.ShapeDtypeStruct((m, width), BF16),
        ),
        grid_spec=pltpu.PrefetchScalarGridSpec(
            num_scalar_prefetch=2,
            grid=(pairs // per,),
            in_specs=[col(n), col(m), col(m), whole(n), whole(m), col(n), col(n), vec],
            out_specs=[col(n), col(m), col(m)],
            scratch_shapes=[
                pltpu.VMEM((n, wide), F32),
                pltpu.VMEM((per, block, LANES), F32),
                pltpu.VMEM((per, block, LANES), F32),
                pltpu.VMEM((per, count, 2 * block, 2 * LANES), BF16),
                pltpu.VMEM((per, count, 2 * block, LANES), BF16),
                pltpu.VMEM((per, count, 1, 2 * block), F32),
            ],
        ),
        compiler_params=pltpu.CompilerParams(vmem_limit_bytes=VMEM_LIMIT),
        cost_estimate=pl.CostEstimate(flops=int(20e9), bytes_accessed=int(12e6), transcendentals=int(4e6)),
        name="attend_back",
    )(lo, hi, q, k, v, fq, fk, g, out, lse)


def norm_forward(summed, gain, shift):
    centred = summed - jnp.mean(summed, axis=-1, keepdims=True)
    inverse = lax.rsqrt(jnp.mean(centred * centred, axis=-1, keepdims=True) + EPSILON)
    normed = centred * inverse
    return normed * gain + shift, normed, inverse


def norm_backward(upstream, normed, inverse, gain):
    scaled = upstream * gain
    first_mean = jnp.mean(scaled, axis=-1, keepdims=True)
    second_mean = jnp.mean(scaled * normed, axis=-1, keepdims=True)
    result = inverse * (scaled - first_mean - normed * second_mean)
    return result, jnp.sum(upstream * normed, axis=0, keepdims=True), jnp.sum(upstream, axis=0, keepdims=True)


CHUNK = 256


def ffn_kernel(
    r2_ref, ct_ref, gains_ref, shifts_ref, up_ref, down_ref,
    acts_ref, slopes_ref, out_ref, dr3_ref, da3_ref, h2b_ref, gs_ref, h2, a3,
):
    step = pl.program_id(0)
    chunks = r2_ref.shape[0] // CHUNK
    rows_of = lambda c: pl.ds(pl.multiple_of(c * CHUNK, CHUNK), CHUNK)

    @pl.when(step == 0)
    def _():
        def first(c, _):
            rows = rows_of(c)
            h, _, _ = norm_forward(r2_ref[rows, :], gains_ref[1:2, :], shifts_ref[1:2, :])
            h2[rows, :] = h
            h2b_ref[rows, :] = h.astype(BF16)
            a3[rows, :] = jnp.zeros_like(h)
            return 0

        lax.fori_loop(0, chunks, first, 0)

    def main(c, _):
        rows = rows_of(c)
        u = dot(h2b_ref[rows, :], up_ref[...], NT)
        phi = 0.5 * (1.0 + lax.erf(u * (2 ** -0.5)))
        act = (u * phi).astype(BF16)
        acts_ref[rows, :] = act
        slopes_ref[rows, :] = (phi + u * jnp.exp(-0.5 * u * u) * ((2 * jnp.pi) ** -0.5)).astype(BF16)
        a3[rows, :] += dot(act, down_ref[...], NN)
        return 0

    lax.fori_loop(0, chunks, main, 0, unroll=True)

    @pl.when(step == pl.num_programs(0) - 1)
    def _():
        def final(c, carry):
            rows = rows_of(c)
            h, normed, inverse = norm_forward(h2[rows, :] + a3[rows, :], gains_ref[2:3, :], shifts_ref[2:3, :])
            out_ref[rows, :] = h.astype(BF16)
            dr, gg, gs = norm_backward(ct_ref[rows, :].astype(F32), normed, inverse, gains_ref[2:3, :])
            dr3_ref[rows, :] = dr
            da3_ref[rows, :] = dr.astype(BF16)
            return carry[0] + gg, carry[1] + gs

        zero = jnp.zeros((1, r2_ref.shape[1]), F32)
        gg, gs = lax.fori_loop(0, chunks, final, (zero, zero))
        gs_ref[...] = jnp.concatenate([gg, gs], axis=0)


def ffn_back_kernel(
    dr3_ref, da3_ref, h2b_ref, r2_ref, gains_ref, acts_ref, slopes_ref, up_ref, down_ref,
    gup_ref, gdown_ref, dr2_ref, da2_ref, gs_ref, du, dh2,
):
    step = pl.program_id(0)
    chunks = dr3_ref.shape[0] // CHUNK
    rows_of = lambda c: pl.ds(pl.multiple_of(c * CHUNK, CHUNK), CHUNK)

    @pl.when(step == 0)
    def _():
        dh2[...] = dr3_ref[...]

    def main(c, _):
        rows = rows_of(c)
        dg = dot(da3_ref[rows, :], down_ref[...], NT)
        d = (slopes_ref[rows, :].astype(F32) * dg).astype(BF16)
        du[rows, :] = d
        dh2[rows, :] += dot(d, up_ref[...], NN)
        return 0

    lax.fori_loop(0, chunks, main, 0, unroll=True)
    gdown_ref[...] = dot(acts_ref[...], da3_ref[...], TN).astype(BF16)
    gup_ref[...] = dot(du[...], h2b_ref[...], TN).astype(BF16)

    @pl.when(step == pl.num_programs(0) - 1)
    def _():
        def final(c, carry):
            rows = rows_of(c)
            r = r2_ref[rows, :]
            _, normed, inverse = norm_forward(r, gains_ref[1:2, :], 0.0)
            dr, gg, gs = norm_backward(dh2[rows, :], normed, inverse, gains_ref[1:2, :])
            dr2_ref[rows, :] = dr
            da2_ref[rows, :] = dr.astype(BF16)
            return carry[0] + gg, carry[1] + gs

        zero = jnp.zeros((1, r2_ref.shape[1]), F32)
        gg, gs = lax.fori_loop(0, chunks, final, (zero, zero))
        gs_ref[...] = jnp.concatenate([gg, gs], axis=0)


FFN_BLOCK = 512


def ffn(r2, ct, gains, shifts, up, down):
    n, width = r2.shape
    hidden = up.shape[0]
    whole = lambda *s: pl.BlockSpec(s, lambda i: (0,) * len(s))
    wblk = pl.BlockSpec((FFN_BLOCK, width), lambda i: (i, 0))
    ablk = pl.BlockSpec((n, FFN_BLOCK), lambda i: (0, i))
    return pl.pallas_call(
        ffn_kernel,
        grid=(hidden // FFN_BLOCK,),
        in_specs=[whole(n, width), whole(n, width), whole(3, width), whole(3, width), wblk, wblk],
        out_specs=[ablk, ablk, whole(n, width), whole(n, width), whole(n, width), whole(n, width), whole(2, width)],
        out_shape=[
            jax.ShapeDtypeStruct((n, hidden), BF16),
            jax.ShapeDtypeStruct((n, hidden), BF16),
            jax.ShapeDtypeStruct((n, width), BF16),
            jax.ShapeDtypeStruct((n, width), F32),
            jax.ShapeDtypeStruct((n, width), BF16),
            jax.ShapeDtypeStruct((n, width), BF16),
            jax.ShapeDtypeStruct((2, width), F32),
        ],
        scratch_shapes=[pltpu.VMEM((n, width), F32), pltpu.VMEM((n, width), F32)],
        compiler_params=pltpu.CompilerParams(vmem_limit_bytes=VMEM_LIMIT),
        cost_estimate=pl.CostEstimate(flops=4 * n * width * hidden, bytes_accessed=int(30e6), transcendentals=2 * n * hidden),
        name="ffn",
    )(r2, ct, gains, shifts, up, down)


def ffn_back(dr3, da3, h2b, r2, gains, acts, slopes, up, down):
    n, width = r2.shape
    hidden = up.shape[0]
    whole = lambda *s: pl.BlockSpec(s, lambda i: (0,) * len(s))
    wblk = pl.BlockSpec((FFN_BLOCK, width), lambda i: (i, 0))
    ablk = pl.BlockSpec((n, FFN_BLOCK), lambda i: (0, i))
    return pl.pallas_call(
        ffn_back_kernel,
        grid=(hidden // FFN_BLOCK,),
        in_specs=[whole(n, width), whole(n, width), whole(n, width), whole(n, width), whole(3, width), ablk, ablk, wblk, wblk],
        out_specs=[wblk, wblk, whole(n, width), whole(n, width), whole(2, width)],
        out_shape=[
            jax.ShapeDtypeStruct((hidden, width), BF16),
            jax.ShapeDtypeStruct((hidden, width), BF16),
            jax.ShapeDtypeStruct((n, width), F32),
            jax.ShapeDtypeStruct((n, width), BF16),
            jax.ShapeDtypeStruct((2, width), F32),
        ],
        scratch_shapes=[pltpu.VMEM((n, FFN_BLOCK), BF16), pltpu.VMEM((n, width), F32)],
        compiler_params=pltpu.CompilerParams(vmem_limit_bytes=VMEM_LIMIT),
        cost_estimate=pl.CostEstimate(flops=8 * n * width * hidden, bytes_accessed=int(40e6), transcendentals=0),
        name="ffn_back",
    )(dr3, da3, h2b, r2, gains, acts, slopes, up, down)


def local_step(x, e, ct, t_ids, s_ids, w, gains, shifts):
    x32 = x.astype(F32)
    q, k, v = [dot(x, w["qkv"][c], NT).astype(BF16) for c in range(3)]
    k2, v2 = [dot(e, w["ckv"][c], NT).astype(BF16) for c in range(2)]
    fq, fk = seg_features(t_ids, t_ids)
    _, fs = seg_features(t_ids, s_ids)
    ctx1, lse1 = attend(q, k, v, t_ids, t_ids, fq, fk, True)
    h1, n1, i1 = norm_forward(x32 + dot(ctx1, w["out"], NN), gains[0], shifts[0])
    h1b = h1.astype(BF16)
    q2 = dot(h1b, w["cq"], NT).astype(BF16)
    ctx2, lse2 = attend(q2, k2, v2, t_ids, s_ids, fq, fs, False)
    r2 = h1 + dot(ctx2, w["cout"], NN)
    acts, slopes, layer_out, dr3, da3, h2b, small3 = ffn(r2, ct, gains, shifts, w["up"], w["down"])
    g_up, g_down, dr2, da2, small2 = ffn_back(dr3, da3, h2b, r2, gains, acts, slopes, w["up"], w["down"])
    g_cout = dot(ctx2, da2, TN).astype(BF16)
    dctx2 = dot(da2, w["cout"], NT).astype(BF16)
    dq2, dk2, dv2 = attend_back(q2, k2, v2, dctx2, ctx2, lse2, t_ids, s_ids, fq, fs, False)
    g_cq = dot(dq2, h1b, TN).astype(BF16)
    g_ckv = [dot(dk2, e, TN).astype(BF16), dot(dv2, e, TN).astype(BF16)]
    grad_e = (dot(dk2, w["ckv"][0], NN) + dot(dv2, w["ckv"][1], NN)).astype(BF16)
    dh1 = dr2 + dot(dq2, w["cq"], NN)
    dr1, gg1, gs1 = norm_backward(dh1, n1, i1, gains[0])
    da1 = dr1.astype(BF16)
    g_out = dot(ctx1, da1, TN).astype(BF16)
    dctx1 = dot(da1, w["out"], NT).astype(BF16)
    dq, dk, dv = attend_back(q, k, v, dctx1, ctx1, lse1, t_ids, t_ids, fq, fk, True)
    g_qkv = [dot(d, x, TN).astype(BF16) for d in (dq, dk, dv)]
    grad_x = (dr1 + dot(dq, w["qkv"][0], NN) + dot(dk, w["qkv"][1], NN) + dot(dv, w["qkv"][2], NN)).astype(BF16)
    grads = dict(qkv=g_qkv, out=g_out, cq=g_cq, ckv=g_ckv, cout=g_cout, up=g_up, down=g_down)
    grad_gains = jnp.concatenate([gg1, small2[0:1], small3[0:1]], axis=0)
    grad_shifts = jnp.concatenate([gs1, small2[1:2], small3[1:2]], axis=0)
    return layer_out, grad_x, grad_e, grads, grad_gains, grad_shifts

MESH = pl.DeviceIdType.MESH

def greet(devices):
    barrier = pltpu.get_barrier_semaphore()
    for device in devices:
        pl.semaphore_signal(barrier, inc=1, device_id=device, device_id_type=MESH)
    pl.semaphore_wait(barrier, len(devices))


def gather_kernel(groups, chunks, window, pack_ref, out_ref, local_sem, send_sem, recv_sem):
    p, t = lax.axis_index("dp"), lax.axis_index("tensor")
    rows = pack_ref.shape[1]
    n = rows // chunks
    zs = [jnp.bitwise_xor(t, j) for j in (1, 2, 3)]
    to_c, to_x, to_y = [(jnp.bitwise_xor(p, b), t) for b in (1, 2, 4)]
    far = jnp.bitwise_xor(p, 6)
    greet([to_c, to_x, to_y] + [(p, z) for z in zs])
    keep = pltpu.make_async_copy(pack_ref, out_ref.at[:, t], local_sem)
    keep.start()
    count = [0]
    copies = []

    def send(src, dst, device):
        i = count[0]
        count[0] += 1
        copy = pltpu.make_async_remote_copy(
            src, dst, send_sem.at[i], recv_sem.at[i], device_id=device, device_id_type=MESH
        )
        copy.start()
        copies.append(copy)
        return copy

    cut = lambda c: pl.ds(c * n, n)
    steps = [(g, c) for g in range(groups) for c in range(chunks)]
    z_in, x_in, y_in, xd_in, yd_in = {}, {}, {}, {}, {}
    last = []

    def start_z(i):
        g, c = steps[i]
        a = g * 8 + p
        for j in range(3):
            z_in[i, j] = send(pack_ref.at[a, cut(c)], out_ref.at[a, t, cut(c)], (p, zs[j]))

    def stage_z(i):
        g, c = steps[i]
        for j in range(3):
            z_in[i, j].wait_recv()
            ref = out_ref.at[g * 8 + p, zs[j], cut(c)]
            x_in[i, j] = send(ref, ref, to_x)
            y_in[i, j] = send(ref, ref, to_y)
            last.append(send(ref, ref, to_c))
        if i + window < len(steps):
            start_z(i + window)

    def stage_xy(i):
        g, c = steps[i]
        for j in range(3):
            x_in[i, j].wait_recv()
            ref = out_ref.at[g * 8 + to_x[0], zs[j]]
            part = ref.at[pl.ds(c * n, n // 2)]
            yd_in[i, j] = send(part, part, to_y)
            part = ref.at[cut(c)]
            last.append(send(part, part, to_c))
            y_in[i, j].wait_recv()
            ref = out_ref.at[g * 8 + to_y[0], zs[j]]
            part = ref.at[pl.ds(c * n + n // 2, n // 2)]
            xd_in[i, j] = send(part, part, to_x)
            part = ref.at[cut(c)]
            last.append(send(part, part, to_c))

    def stage_far(i):
        g, c = steps[i]
        for j in range(3):
            xd_in[i, j].wait_recv()
            yd_in[i, j].wait_recv()
            ref = out_ref.at[g * 8 + far, zs[j], cut(c)]
            last.append(send(ref, ref, to_c))

    for i in range(window):
        start_z(i)
    stages = (stage_z, stage_xy, stage_far)
    for step in range(len(steps) + 2):
        for k in (2, 1, 0):
            if 0 <= step - k < len(steps):
                stages[k](step - k)
    for copy in last:
        copy.wait_recv()
    for copy in copies:
        copy.wait_send()
    keep.wait()


def gather_pack(pack, collective_id, chunks=3, window=1):
    mats, rows, width = pack.shape
    groups = mats // 8
    count = groups * chunks * (3 + 9 + 3 * 2 + 3 * 2 + 3)
    return pl.pallas_call(
        functools.partial(gather_kernel, groups, chunks, window),
        out_shape=jax.ShapeDtypeStruct((mats, 4, rows, width), pack.dtype),
        in_specs=[pl.BlockSpec(memory_space=pltpu.VMEM)],
        out_specs=pl.BlockSpec(memory_space=pl.ANY),
        scratch_shapes=[
            pltpu.SemaphoreType.DMA,
            pltpu.SemaphoreType.DMA((count,)),
            pltpu.SemaphoreType.DMA((count,)),
        ],
        compiler_params=pltpu.CompilerParams(collective_id=collective_id, has_side_effects=True, vmem_limit_bytes=32 * 2**20),
        name="gather_pack",
    )(pack)


def reduce_kernel(chunks, mats, *refs):
    grads, small_ref = refs[:mats], refs[mats]
    (out_ref, small_out_ref, mine, from_c, from_x1, from_y1, from_x2, from_y2, from_z, piece,
     s_send, s_c, s_x, s_y, s_z, local_sem, send_sem, recv_sem, small_send, small_recv) = refs[mats + 1 :]
    p, t = lax.axis_index("dp"), lax.axis_index("tensor")
    half = grads[0].shape[1] // 2
    n = half // chunks
    per = mats // 4
    core, cx, cy = lax.rem(p, 2), lax.rem(p // 2, 2), p // 4
    chip = p // 2
    zs = [jnp.bitwise_xor(t, j) for j in (1, 2, 3)]
    to_c, to_x, to_y = [(jnp.bitwise_xor(p, b), t) for b in (1, 2, 4)]
    greet([to_c, to_x, to_y] + [(p, z) for z in zs])
    count = [0]
    copies = []

    def send(src, dst, device):
        i = count[0]
        count[0] += 1
        copy = pltpu.make_async_remote_copy(
            src, dst, send_sem.at[i], recv_sem.at[i], device_id=device, device_id_type=MESH
        )
        copy.start()
        copies.append(copy)
        return copy

    small_count = [0]

    def send_small(src, dst, device):
        i = small_count[0]
        small_count[0] += 1
        copy = pltpu.make_async_remote_copy(
            src, dst, small_send.at[i], small_recv.at[i], device_id=device, device_id_type=MESH
        )
        copy.start()
        return copy

    nx, ny = 1 - cx, 1 - cy
    c_in, x1, y1, x2, y2, z_in, gx, gy, gxd, gyd, last = {}, {}, {}, {}, {}, {}, {}, {}, {}, {}, []
    local = {}
    cut = lambda c: pl.ds(c * n, n)
    own_cut = lambda c: pl.ds(pl.multiple_of(core * half + c * n, 16), n)
    other_cut = lambda c: pl.ds(pl.multiple_of((1 - core) * half + c * n, 16), n)
    owned = lambda q: pl.ds(q * per, per)
    for c in range(chunks):
        c_in[c], local[c] = [], []
        for a in range(mats):
            c_in[c].append(send(grads[a].at[:, other_cut(c)], from_c.at[a, :, cut(c)], to_c))
            copy = pltpu.make_async_copy(
                grads[a].at[:, own_cut(c)], mine.at[a, :, cut(c)], local_sem.at[c * mats + a]
            )
            copy.start()
            local[c].append(copy)
    small = send_small(small_ref, s_c, to_c)

    def add(dst, src):
        dst[...] = (dst[...].astype(F32) + src[...].astype(F32)).astype(dst.dtype)

    def stage_c(c):
        for a in range(mats):
            c_in[c][a].wait_recv()
            local[c][a].wait()
            for b in range(4):
                add(mine.at[a, b, cut(c)], from_c.at[a, b, cut(c)])
        x1[c] = [send(mine.at[owned(q * 2 + nx), 0:2, cut(c)], from_x1.at[q, :, :, cut(c)], to_x) for q in range(2)]
        y1[c] = [send(mine.at[owned(ny * 2 + q), 2:4, cut(c)], from_y1.at[q, :, :, cut(c)], to_y) for q in range(2)]

    def stage_xy(c):
        for q in range(2):
            x1[c][q].wait_recv()
            for i in range(per):
                for b in range(2):
                    add(mine.at[(q * 2 + cx) * per + i, b, cut(c)], from_x1.at[q, i, b, cut(c)])
        x2[c] = send(mine.at[owned(ny * 2 + cx), 0:2, cut(c)], from_x2.at[:, :, cut(c)], to_y)
        for q in range(2):
            y1[c][q].wait_recv()
            for i in range(per):
                for b in range(2):
                    add(mine.at[(cy * 2 + q) * per + i, 2 + b, cut(c)], from_y1.at[q, i, b, cut(c)])
        y2[c] = send(mine.at[owned(cy * 2 + nx), 2:4, cut(c)], from_y2.at[:, :, cut(c)], to_x)

    def stage_z(c):
        x2[c].wait_recv()
        for i in range(per):
            for b in range(2):
                add(mine.at[chip * per + i, b, cut(c)], from_x2.at[i, b, cut(c)])
        y2[c].wait_recv()
        for i in range(per):
            for b in range(2):
                add(mine.at[chip * per + i, 2 + b, cut(c)], from_y2.at[i, b, cut(c)])
        z_in[c] = [
            send(mine.at[owned(chip), zs[j], cut(c)], from_z.at[j, :, cut(c)], (p, zs[j])) for j in range(3)
        ]

    def stage_out(c):
        for j in range(3):
            z_in[c][j].wait_recv()
        for i in range(per):
            total = mine[chip * per + i, t, cut(c), :].astype(F32)
            for j in range(3):
                total = total + from_z[j, i, cut(c), :].astype(F32)
            piece[chip * per + i, own_cut(c), :] = total.astype(piece.dtype)
        ref = piece.at[owned(chip), own_cut(c)]
        gx[c] = send(ref, ref, to_x)
        gy[c] = send(ref, ref, to_y)
        last.append(send(ref, ref, to_c))

    def stage_far(c):
        gx[c].wait_recv()
        ref = piece.at[owned(cy * 2 + nx), own_cut(c)]
        gyd[c] = send(ref.at[: per // 2], ref.at[: per // 2], to_y)
        last.append(send(ref, ref, to_c))
        gy[c].wait_recv()
        ref = piece.at[owned(ny * 2 + cx), own_cut(c)]
        gxd[c] = send(ref.at[per // 2 :], ref.at[per // 2 :], to_x)
        last.append(send(ref, ref, to_c))

    def stage_end(c):
        gxd[c].wait_recv()
        gyd[c].wait_recv()
        ref = piece.at[owned(ny * 2 + nx), own_cut(c)]
        last.append(send(ref, ref, to_c))

    stages = (stage_c, stage_xy, stage_z, stage_out, stage_far, stage_end)
    for step in range(chunks + len(stages) - 1):
        for k in reversed(range(len(stages))):
            if 0 <= step - k < chunks:
                stages[k](step - k)
        if step == 0:
            small.wait()
            s_send[0] = small_ref[...] + s_c[...]
            small = send_small(s_send.at[0], s_x, to_x)
        elif step == 1:
            small.wait()
            s_send[1] = s_send[0] + s_x[...]
            small = send_small(s_send.at[1], s_y, to_y)
        elif step == 2:
            small.wait()
            s_send[2] = s_send[1] + s_y[...]
            s_z[t] = s_send[2]
            small = [send_small(s_send.at[2], s_z.at[t], (p, z)) for z in zs]
    for copy in small:
        copy.wait()
    small_out_ref[...] = (s_z[0] + s_z[1]) + (s_z[2] + s_z[3])
    for copy in last:
        copy.wait_recv()
    for copy in copies:
        copy.wait_send()
    for a in range(mats):
        out_ref[a] = piece[a].astype(out_ref.dtype)


def reduce_pack(grads, small, collective_id, chunks=3):
    mats = len(grads)
    tensor, rows, width = grads[0].shape
    half, per = rows // 2, mats // 4
    count = chunks * (mats + 4 + 2 + 3 + 3 + 4 + 1)
    vmem = pl.BlockSpec(memory_space=pltpu.VMEM)
    buf = lambda *s: pltpu.VMEM(s + (half, width), BF16)
    sb = lambda *s: pltpu.VMEM(s + small.shape, F32)
    return pl.pallas_call(
        functools.partial(reduce_kernel, chunks, mats),
        out_shape=(jax.ShapeDtypeStruct((mats, rows, width), F32), jax.ShapeDtypeStruct(small.shape, F32)),
        in_specs=[pl.BlockSpec(memory_space=pl.ANY)] * mats + [vmem],
        out_specs=(vmem, vmem),
        scratch_shapes=[
            buf(mats, 4), buf(mats, 4), buf(2, per, 2), buf(2, per, 2), buf(per, 2), buf(per, 2), buf(3, per),
            pltpu.VMEM((mats, rows, width), BF16),
            sb(3), sb(), sb(), sb(), sb(4),
            pltpu.SemaphoreType.DMA((chunks * mats,)),
            pltpu.SemaphoreType.DMA((count,)),
            pltpu.SemaphoreType.DMA((count,)),
            pltpu.SemaphoreType.DMA((6,)),
            pltpu.SemaphoreType.DMA((6,)),
        ],
        compiler_params=pltpu.CompilerParams(
            collective_id=collective_id, has_side_effects=True, vmem_limit_bytes=48 * 2**20
        ),
        cost_estimate=pl.CostEstimate(flops=int(1e9), bytes_accessed=int(60e6), transcendentals=0),
        name="reduce_pack",
    )(*grads, small)


def gather_rows(shard):
    mats, rows, width = shard.shape
    dp, tensor = lax.axis_size("dp"), lax.axis_size("tensor")
    if (dp, tensor, mats) == (8, 4, 8):
        return gather_pack(shard, 0).reshape(mats, tensor * rows, width)
    piece = mats * rows // dp
    mine = lax.dynamic_slice_in_dim(
        shard.reshape(mats * rows, width), lax.axis_index("dp") * piece, piece, 0
    )
    full = lax.all_gather(mine, ("dp", "tensor"), axis=0, tiled=True)
    full = full.reshape(mats, dp // mats, tensor, piece, width).transpose(0, 2, 1, 3, 4)
    return full.reshape(mats, tensor * rows, width)


def reduce_rows(grads, small):
    mats = len(grads)
    all_rows, width = grads[0].shape
    dp, tensor = lax.axis_size("dp"), lax.axis_size("tensor")
    rows = all_rows // tensor
    if (dp, tensor, mats) == (8, 4, 8):
        return reduce_pack([g.reshape(tensor, rows, width) for g in grads], small, 1)
    piece = mats * rows // dp
    grad = jnp.stack(grads).reshape(mats, tensor, dp // mats, piece, width).transpose(0, 2, 1, 3, 4)
    mine = lax.psum_scatter(
        grad.reshape(dp * tensor * piece, width), ("dp", "tensor"), scatter_dimension=0, tiled=True
    )
    total = lax.all_gather(mine, "dp", axis=0, tiled=True).reshape(mats, rows, width).astype(F32)
    return total, lax.psum(small, ("dp", "tensor"))


def per_device(
    inputs, encoded, cotangent, tgt_seg, src_seg, self_qkv, self_out, cross_q, cross_kv, cross_out, ffn_up, ffn_down, gains, shifts
):
    me = lax.axis_index("tensor")
    t_ids = lax.dynamic_index_in_dim(tgt_seg, me, 0, keepdims=False)
    s_ids = lax.dynamic_index_in_dim(src_seg, me, 0, keepdims=False)
    pack = jnp.concatenate(
        [
            self_qkv.transpose(0, 2, 1),
            self_out[None],
            cross_q.T[None],
            cross_kv.transpose(0, 2, 1),
            cross_out[None],
        ],
        axis=0,
    )
    pack = gather_rows(pack)
    hidden = ffn_down.shape[0]
    width = inputs.shape[1]
    dp, tensor = lax.axis_size("dp"), lax.axis_size("tensor")
    piece = hidden // dp
    start = lax.axis_index("dp") * piece
    up, down = [
        lax.all_gather(lax.dynamic_slice_in_dim(m, start, piece, 0), ("dp", "tensor"), axis=0, tiled=True)
        for m in (ffn_up.T, ffn_down)
    ]
    w = dict(qkv=pack[0:3], out=pack[3], cq=pack[4], ckv=pack[5:7], cout=pack[7], up=up, down=down)
    layer_out, grad_x, grad_e, grads, grad_gains, grad_shifts = local_step(
        inputs, encoded, cotangent, t_ids, s_ids, w, gains, shifts
    )
    g_up, g_down = [
        lax.all_gather(
            lax.psum_scatter(grads[name], ("dp", "tensor"), scatter_dimension=0, tiled=True), "dp", axis=0, tiled=True
        )
        for name in ("up", "down")
    ]
    small = jnp.concatenate([grad_gains, grad_shifts, jnp.zeros((2, width), F32)], axis=0)
    total, small = reduce_rows(
        [*grads["qkv"], grads["out"], grads["cq"], *grads["ckv"], grads["cout"]], small
    )
    return (
        layer_out,
        grad_x,
        grad_e,
        total[0:3].transpose(0, 2, 1),
        total[3],
        total[4].T,
        total[5:7].transpose(0, 2, 1),
        total[7],
        g_up.astype(F32).T,
        g_down.astype(F32),
        small[0:3],
        small[3:6],
    )


def solution(mesh):
    rows = P(("dp", "tensor"), None)
    in_specs = (
        rows, rows, rows, P("dp", None), P("dp", None),
        P(None, None, "tensor"), P("tensor", None), P(None, "tensor"), P(None, None, "tensor"), P("tensor", None),
        P(None, "tensor"), P("tensor", None), P(), P(),
    )
    out_specs = (
        rows, rows, rows,
        P(None, None, "tensor"), P("tensor", None), P(None, "tensor"), P(None, None, "tensor"), P("tensor", None),
        P(None, "tensor"), P("tensor", None), P(), P(),
    )
    return jax.shard_map(per_device, mesh=mesh, in_specs=in_specs, out_specs=out_specs, check_vma=False)
```

profile of v0, /device:TPU:0, one launch (start us, length us, event | category | flops | bytes accessed | tf_op | source)
XLA Modules:
  0.0 493.3 jit_solution(7001198975528279935)
XLA Ops:
  15.5 50.6 %gather_pack.1 = bf16[8,4,192,768]{3,2,1,0:T(8,128)(2,1)S(1)} custom-call(bf16[8,192,768]{2,1,0:T(8,128)(2,1)S(1)} %bitcast_dynamic-update-slice_fusion.3.pack_ref), custom_call_target="tpu_custom_call" | custom-call | tf_op jit(solution)/shard_map/gather_pack/pallas_call | solution.py:534
  72.3 3.0 fusion.2.q_ref
  80.5 16.2 %attend.2 = (bf16[1024,768]{1,0:T(8,128)(2,1)}, f32[6,4,1,512]{3,2,1,0:T(1,128)}) custom-call(s32[4]{0:T(128)} %get-tuple-element.153.lo_ref, s32[4]{0:T(128)} %get-tuple-element.152.hi_ref, bf16[1024,768]{1,0:T(8,128)(2,1)} %fusion.2.q_ref, bf16[1024,768]{1,0:T(8,128)(2,1)} %fusion.3.k_ref, bf16[1024,768]{1,0:T(8,128)(2,1)} %fusion.4.v_ref, ...), custom_call_target="tpu_custom_call" | custom-call | flops 8000000000 | bytes 8000000 | tf_op jit(solution)/shard_map/attend/pallas_call | solution.py:188
  96.7 3.4 fusion.20
  109.8 19.1 %attend.3 = (bf16[1024,768]{1,0:T(8,128)(2,1)}, f32[6,4,1,512]{3,2,1,0:T(1,128)}) custom-call(s32[4]{0:T(128)} %get-tuple-element.151.lo_ref, s32[4]{0:T(128)} %get-tuple-element.150.hi_ref, bf16[1024,768]{1,0:T(8,128)(2,1)} %convolution_convert_fusion.4.q_ref, bf16[1024,768]{1,0:T(8,128)(2,1)} %fusion.5.k_ref, bf16[1024,768]{1,0:T(8,128)(2,1)} %fusion.6.v_ref, ...), custom_call_target="tpu_custom_call" | custom-call | flops 8000000000 | bytes 8000000 | tf_op jit(solution)/shard_map/attend/pallas_call | solution.py:188
  128.9 4.5 fusion.r2_ref
  133.4 17.9 %all-gather.7.cloned.1.call-done.down_ref = bf16[3072,768]{1,0:T(8,128)(2,1)} async-done(((bf16[96,768]{1,0:T(8,128)(2,1)}), bf16[3072,768]{1,0:T(8,128)(2,1)}) %all-gather.7.cloned.1.call-update) | async-done | bytes 4718608 | tf_op jit(solution)/shard_map/all_gather | solution.py:785
  151.3 25.4 %ffn.1 = (bf16[1024,3072]{1,0:T(8,128)(2,1)}, bf16[1024,3072]{1,0:T(8,128)(2,1)}, bf16[1024,768]{1,0:T(8,128)(2,1)}, f32[1024,768]{1,0:T(8,128)}, bf16[1024,768]...) custom-call(f32[1024,768]{1,0:T(8,128)} %fusion.r2_ref, bf16[1024,768]{1,0:T(8,128)(2,1)} %ct_ref.1, ...), custom_call_target="tpu_custom_call" | custom-call | flops 9663676416 | bytes 30000000 | tf_op jit(solution)/shard_map/ffn/pallas_call | solution.py:359
  176.7 33.3 %ffn_back.1 = (bf16[3072,768]{1,0:T(8,128)(2,1)}, bf16[3072,768]{1,0:T(8,128)(2,1)}, f32[1024,768]{1,0:T(8,128)}, bf16[1024,768]{1,0:T(8,128)(2,1)}, f32[2,768]{1,0:T(2,128)}) custom-call(f32[1024,768]{1,0:T(8,128)} %get-tuple-element.39.dr3_ref, bf16[1024,768]{1,0:T(8,128)(2,1)} %get-tuple-element.40.da3_ref, bf16[1024,768]{1,0:T(8,128)(2,1)} %get-tuple-element.41.h2b_ref, ...), custom_call_target="tpu_custom_call" | custom-call | flops 19327352832 | bytes 40000000 | tf_op jit(solution)/shard_map/ffn_back/pallas_call | solution.py:386
  210.8 4.3 convolution_convert_fusion.1.g_ref
  215.1 30.0 %attend_back.2 = (bf16[1024,768]{1,0:T(8,128)(2,1)}, bf16[1024,768]{1,0:T(8,128)(2,1)}, bf16[1024,768]{1,0:T(8,128)(2,1)}) custom-call(s32[4]{0:T(128)} %get-tuple-element.149.lo_ref, s32[4]{0:T(128)} %get-tuple-element.148.hi_ref, bf16[1024,768]{1,0:T(8,128)(2,1)} %convolution_convert_fusion.4.q_ref, bf16[1024,768]{1,0:T(8,128)(2,1)} %fusion.5.k_ref, ...), custom_call_target="tpu_custom_call" | custom-call | flops 20000000000 | bytes 12000000 | tf_op jit(solution)/shard_map/attend_back/pallas_call | solution.py:217
  245.1 6.1 %multiply_reduce_fusion = (f32[768]{0:T(1024)S(1)}, f32[1024]{0:T(1024)S(1)}, f32[1024]{0:T(1024)S(1)}, f32[768]{0:T(1024)S(1)}, f32[1024,768]{1,0:T(8,128)}) fusion(f32[1024,768]{1,0:T(8,128)S(1)} %copy-done.6, f32[1024]{0:T(1024)S(1)} %add_rsqrt_fusion, f32[1024]{0:T(1024)S(1)} %broadcast_multiply_fusion.2, f32[768]{0:T(1024)S(1)} %get-tuple-element.155, ...), kind=kOutput, calls=%fused_computation | convolution fusion | flops 1215820288 | bytes 12215296 | tf_op jit(solution)/shard_map/dot_general | solution.py:20
  252.1 4.5 convolution_convert_fusion.8
  260.2 25.9 %attend_back.3 = (bf16[1024,768]{1,0:T(8,128)(2,1)}, bf16[1024,768]{1,0:T(8,128)(2,1)}, bf16[1024,768]{1,0:T(8,128)(2,1)}) custom-call(s32[4]{0:T(128)} %get-tuple-element.153.lo_ref, s32[4]{0:T(128)} %get-tuple-element.152.hi_ref, bf16[1024,768]{1,0:T(8,128)(2,1)} %fusion.2.q_ref, bf16[1024,768]{1,0:T(8,128)(2,1)} %fusion.3.k_ref, ...), custom_call_target="tpu_custom_call" | custom-call | flops 20000000000 | bytes 12000000 | tf_op jit(solution)/shard_map/attend_back/pallas_call | solution.py:217
  286.2 3.0 convolution_convert_fusion.15
  301.8 14.1 %reduce-scatter.3.cloned.1.call-done = bf16[96,768]{1,0:T(8,128)(2,1)} async-done(((bf16[3072,768]{1,0:T(8,128)(2,1)}), bf16[96,768]{1,0:T(8,128)(2,1)}) %reduce-scatter.3.cloned.1.call-update) | async-done | bytes 147472 | tf_op jit(solution)/shard_map/reduce_scatter | solution.py:794
  316.0 4.0 convolution_convert_fusion.9
  320.1 78.0 %reduce_pack.1 = (f32[8,192,768]{2,1,0:T(8,128)}, f32[8,768]{1,0:T(8,128)S(1)}) custom-call(bf16[4,192,768]{2,1,0:T(8,128)(2,1)S(1)} %bitcast.99, bf16[4,192,768]{2,1,0:T(8,128)(2,1)S(1)} %bitcast.100, bf16[4,192,768]{2,1,0:T(8,128)(2,1)S(1)} %bitcast.101, bf16[4,192,768]{2,1,0:T(8,128)(2,1)S(1)} %bitcast.102, bf16[4,192,768]{2,1,0:T(8,128)(2,1)S(1)} %bitcast.103, ...), custom_call_target="tpu_custom_call" | custom-call | flops 1000000000 | bytes 60000000 | tf_op jit(solution)/shard_map/reduce_pack/pallas_call | solution.py:709
  406.1 3.2 fusion.23
  409.3 3.1 fusion.21
  412.3 20.4 %reduce-scatter.5.cloned.1.call-done = bf16[96,768]{1,0:T(8,128)(2,1)} async-done(((bf16[3072,768]{1,0:T(8,128)(2,1)}), bf16[96,768]{1,0:T(8,128)(2,1)}) %reduce-scatter.5.cloned.1.call-update) | async-done | bytes 147472 | tf_op jit(solution)/shard_map/reduce_scatter | solution.py:794
  443.0 14.6 %all-gather.9.cloned.1.call-done = bf16[768,768]{1,0:T(8,128)(2,1)} async-done(((bf16[96,768]{1,0:T(8,128)(2,1)}), bf16[768,768]{1,0:T(8,128)(2,1)}) %all-gather.9.cloned.1.call-update) | async-done | bytes 1179664 | tf_op jit(solution)/shard_map/all_gather | solution.py:793
  460.5 3.0 copy.57
  463.5 19.9 %all-gather.11.cloned.1.call-done = bf16[768,768]{1,0:T(8,128)(2,1)} async-done(((bf16[96,768]{1,0:T(8,128)(2,1)}), bf16[768,768]{1,0:T(8,128)(2,1)}) %all-gather.11.cloned.1.call-update) | async-done | bytes 1179664 | tf_op jit(solution)/shard_map/all_gather | solution.py:793
  (162 shorter events, 70.9 us)
Async XLA Ops:
  7.2 94.7 %copy-start = (bf16[1024,768]{1,0:T(8,128)(2,1)S(1)}, bf16[1024,768]{1,0:T(8,128)(2,1)}, u32[]{:S(2)}) copy-start(bf16[1024,768]{1,0:T(8,128)(2,1)} %param.15) | copy-start | bytes 4718596
  7.2 7.2 %copy-start.28 = (bf16[3,768,192]{1,2,0:T(8,128)(2,1)S(1)}, bf16[3,768,192]{1,2,0:T(8,128)(2,1)}, u32[]{:S(2)}) copy-start(bf16[3,768,192]{1,2,0:T(8,128)(2,1)} %param.19) | copy-start | bytes 2654212
  7.2 126.2 %all-gather.5.cloned.1.call-start = ((), (), s32[]{:S(2)}) async-start(), calls=%async_computation.2 | async-start | bytes 4866048 | tf_op jit(solution)/shard_map/all_gather | solution.py:785
  7.3 7.2 %copy-start.30 = (bf16[192,768]{1,0:T(8,128)(2,1)S(1)}, bf16[192,768]{1,0:T(8,128)(2,1)}, u32[]{:S(2)}) copy-start(bf16[192,768]{1,0:T(8,128)(2,1)} %param.20) | copy-start | bytes 884740
  9.4 141.9 %all-gather.7.cloned.1.call-start = ((), (), s32[]{:S(2)}) async-start(), calls=%async_computation.3 | async-start | bytes 4866048 | tf_op jit(solution)/shard_map/all_gather | solution.py:785
  11.0 4.4 copy-start.29
  11.0 304.9 %reduce-scatter.3.cloned.1.call-start = ((), (), s32[]{:S(2)}) async-start(), calls=%async_computation.4 | async-start | bytes 4866048 | tf_op jit(solution)/shard_map/reduce_scatter | solution.py:794
  72.3 5.6 %copy-start.11 = (bf16[1,4,192,768]{3,2,1,0:T(8,128)(2,1)}, bf16[1,4,192,768]{3,2,1,0:T(8,128)(2,1)S(1)}, u32[]{:S(2)}) copy-start(bf16[1,4,192,768]{3,2,1,0:T(8,128)(2,1)S(1)} %get-tuple-element.133) | copy-start | bytes 3538948
  72.3 29.6 %copy-start.23 = (bf16[1,4,192,768]{3,2,1,0:T(8,128)(2,1)}, bf16[1,4,192,768]{3,2,1,0:T(8,128)(2,1)S(1)}, u32[]{:S(2)}) copy-start(bf16[1,4,192,768]{3,2,1,0:T(8,128)(2,1)S(1)} %get-tuple-element.130) | copy-start | bytes 3538948
  72.3 32.2 %copy-start.17 = (bf16[1,4,192,768]{3,2,1,0:T(8,128)(2,1)}, bf16[1,4,192,768]{3,2,1,0:T(8,128)(2,1)S(1)}, u32[]{:S(2)}) copy-start(bf16[1,4,192,768]{3,2,1,0:T(8,128)(2,1)S(1)} %get-tuple-element.129) | copy-start | bytes 3538948
  100.1 28.8 %copy-start.5 = (f32[1024,768]{1,0:T(8,128)}, f32[1024,768]{1,0:T(8,128)S(1)}, u32[]{:S(2)}) copy-start(f32[1024,768]{1,0:T(8,128)S(1)} %get-tuple-element.146) | copy-start | bytes 9437188
  109.8 19.1 %copy-start.27 = (bf16[1,4,192,768]{3,2,1,0:T(8,128)(2,1)S(1)}, bf16[1,4,192,768]{3,2,1,0:T(8,128)(2,1)}, u32[]{:S(2)}) copy-start(bf16[1,4,192,768]{3,2,1,0:T(8,128)(2,1)} %get-tuple-element.128) | copy-start | bytes 3538948
  210.0 222.8 %reduce-scatter.5.cloned.1.call-start = ((), (), s32[]{:S(2)}) async-start(), calls=%async_computation.6 | async-start | bytes 4866048 | tf_op jit(solution)/shard_map/reduce_scatter | solution.py:794
  215.1 30.0 %copy-start.6 = (f32[1024,768]{1,0:T(8,128)S(1)}, f32[1024,768]{1,0:T(8,128)}, u32[]{:S(2)}) copy-start(f32[1024,768]{1,0:T(8,128)} %copy-done.5) | copy-start | bytes 9437188
  215.1 30.0 %copy-start.26 = (bf16[1,4,192,768]{3,2,1,0:T(8,128)(2,1)S(1)}, bf16[1,4,192,768]{3,2,1,0:T(8,128)(2,1)}, u32[]{:S(2)}) copy-start(bf16[1,4,192,768]{3,2,1,0:T(8,128)(2,1)} %get-tuple-element.131) | copy-start | bytes 3538948
  245.1 6.2 %copy-start.34 = (f32[2,768]{1,0:T(2,128)S(1)}, f32[2,768]{1,0:T(2,128)}, u32[]{:S(2)}) copy-start(f32[2,768]{1,0:T(2,128)} %get-tuple-element.54) | copy-start | bytes 18436
  251.3 206.3 %all-gather.9.cloned.1.call-start = ((), (), s32[]{:S(2)}) async-start(), calls=%async_computation.5 | async-start | bytes 1327104 | tf_op jit(solution)/shard_map/all_gather | solution.py:793
  252.0 4.5 copy-start.7
  252.1 4.5 copy-start.13
  260.2 25.9 %copy-start.36 = (bf16[1024,768]{1,0:T(8,128)(2,1)S(1)}, bf16[1024,768]{1,0:T(8,128)(2,1)}, u32[]{:S(2)}) copy-start(bf16[1024,768]{1,0:T(8,128)(2,1)} %param.14) | copy-start | bytes 4718596
  315.9 167.5 %all-gather.11.cloned.1.call-start = ((), (), s32[]{:S(2)}) async-start(), calls=%async_computation.7 | async-start | bytes 1327104 | tf_op jit(solution)/shard_map/all_gather | solution.py:793
  316.0 4.1 copy-start.1
  409.3 24.1 %copy-start.20 = (bf16[1,4,192,768]{3,2,1,0:T(8,128)(2,1)S(1)}, bf16[1,4,192,768]{3,2,1,0:T(8,128)(2,1)}, u32[]{:S(2)}) copy-start(bf16[1,4,192,768]{3,2,1,0:T(8,128)(2,1)} %copy-done.19) | copy-start | bytes 3538948
  433.4 5.7 %copy-start.16 = (bf16[1024,768]{1,0:T(8,128)(2,1)S(1)}, bf16[1024,768]{1,0:T(8,128)(2,1)}, u32[]{:S(2)}) copy-start(bf16[1024,768]{1,0:T(8,128)(2,1)} %get-tuple-element.51) | copy-start | bytes 4718596
  (28 other events, 76.8 us)
Sparse Core Ops, SparseCore 0:
  11.4 74.6 all-gather.4
  88.9 62.3 all-gather.6
  210.1 105.7 reduce-scatter.2
  322.1 110.5 reduce-scatter.4
  434.5 23.1 all-gather.8
  459.4 24.0 all-gather.10
where the time goes:
time: 502 us; the launch traced here: 493 us
  Pallas kernels  279 us (56%)
  waiting for transfers between devices  87.1 us (17%)
  matrix products  75.3 us (15%)
  local copies, waits for them, and re-layouts  24.9 us (5%)
  between operations  14.8 us (3%)
  other arithmetic  12.2 us (2%)
    pallas_call x1, Pallas kernels, reduce_pack(): pl.pallas_call(functools.partial(reduce_kernel, chunks, mats), out_shape=...  78 us
    dot_general x24, matrix products, dot(): return lax.dot_general(a, b, dims, preferred_element_type=F32)  75.3 us
    pallas_call x2, Pallas kernels, attend_back(): pl.pallas_call(functools.partial(attend_back_kernel, causal, block, per),...  55.9 us
    pallas_call x1, Pallas kernels, gather_pack(): pl.pallas_call(functools.partial(gather_kernel, groups, chunks, window),...  50.6 us
    pallas_call x2, Pallas kernels, attend(): pl.pallas_call(functools.partial(attend_kernel, causal, block, per), out_...  35.3 us
    all_gather x2, waiting for transfers between devices, per_device(): lax.all_gather(lax.psum_scatter(grads[name], ('dp', 'tensor'), scatter_di...  34.6 us
    reduce_scatter x2, waiting for transfers between devices, per_device(): lax.psum_scatter(grads[name], ('dp', 'tensor'), scatter_dimension=0, tile...  34.5 us
    pallas_call x1, Pallas kernels, ffn_back(): pl.pallas_call(ffn_back_kernel, grid=(hidden // FFN_BLOCK,), in_specs=[wh...  33.3 us
  transfers between devices with their start and end apart: 6, of which 5 were waited for; matrix products, arithmetic and copies ran while one was open for 21% of the time, Pallas kernels for 45%

commit v1 on v0

--- a/solution.py
+++ b/solution.py
@@ -172,7 +172,7 @@
 
 
 VMEM_LIMIT = 56 * 2**20
-FWD_PER = 6
+FWD_PER = 3
 BWD_PER = 3
 
 
@@ -260,7 +260,7 @@
 
 
 def ffn_kernel(
-    r2_ref, ct_ref, gains_ref, shifts_ref, up_ref, down_ref,
+    r2_ref, ct_ref, gains_ref, shifts_ref, w_ref,
     acts_ref, slopes_ref, out_ref, dr3_ref, da3_ref, h2b_ref, gs_ref, h2, a3,
 ):
     step = pl.program_id(0)
@@ -281,12 +281,12 @@
 
     def main(c, _):
         rows = rows_of(c)
-        u = dot(h2b_ref[rows, :], up_ref[...], NT)
+        u = dot(h2b_ref[rows, :], w_ref[0], NT)
         phi = 0.5 * (1.0 + lax.erf(u * (2 ** -0.5)))
         act = (u * phi).astype(BF16)
         acts_ref[rows, :] = act
         slopes_ref[rows, :] = (phi + u * jnp.exp(-0.5 * u * u) * ((2 * jnp.pi) ** -0.5)).astype(BF16)
-        a3[rows, :] += dot(act, down_ref[...], NN)
+        a3[rows, :] += dot(act, w_ref[1], NN)
         return 0
 
     lax.fori_loop(0, chunks, main, 0, unroll=True)
@@ -308,8 +308,8 @@
 
 
 def ffn_back_kernel(
-    dr3_ref, da3_ref, h2b_ref, r2_ref, gains_ref, acts_ref, slopes_ref, up_ref, down_ref,
-    gup_ref, gdown_ref, dr2_ref, da2_ref, gs_ref, du, dh2,
+    dr3_ref, da3_ref, h2b_ref, r2_ref, gains_ref, acts_ref, slopes_ref, w_ref,
+    g_ref, dr2_ref, da2_ref, gs_ref, du, dh2,
 ):
     step = pl.program_id(0)
     chunks = dr3_ref.shape[0] // CHUNK
@@ -321,15 +321,15 @@
 
     def main(c, _):
         rows = rows_of(c)
-        dg = dot(da3_ref[rows, :], down_ref[...], NT)
+        dg = dot(da3_ref[rows, :], w_ref[1], NT)
         d = (slopes_ref[rows, :].astype(F32) * dg).astype(BF16)
         du[rows, :] = d
-        dh2[rows, :] += dot(d, up_ref[...], NN)
+        dh2[rows, :] += dot(d, w_ref[0], NN)
         return 0
 
     lax.fori_loop(0, chunks, main, 0, unroll=True)
-    gdown_ref[...] = dot(acts_ref[...], da3_ref[...], TN).astype(BF16)
-    gup_ref[...] = dot(du[...], h2b_ref[...], TN).astype(BF16)
+    g_ref[1] = dot(acts_ref[...], da3_ref[...], TN).astype(BF16)
+    g_ref[0] = dot(du[...], h2b_ref[...], TN).astype(BF16)
 
     @pl.when(step == pl.num_programs(0) - 1)
     def _():
@@ -350,16 +350,16 @@
 FFN_BLOCK = 512
 
 
-def ffn(r2, ct, gains, shifts, up, down):
+def ffn(r2, ct, gains, shifts, w):
     n, width = r2.shape
-    hidden = up.shape[0]
+    hidden = w.shape[1]
     whole = lambda *s: pl.BlockSpec(s, lambda i: (0,) * len(s))
-    wblk = pl.BlockSpec((FFN_BLOCK, width), lambda i: (i, 0))
+    wblk = pl.BlockSpec((2, FFN_BLOCK, width), lambda i: (0, i, 0))
     ablk = pl.BlockSpec((n, FFN_BLOCK), lambda i: (0, i))
     return pl.pallas_call(
         ffn_kernel,
         grid=(hidden // FFN_BLOCK,),
-        in_specs=[whole(n, width), whole(n, width), whole(3, width), whole(3, width), wblk, wblk],
+        in_specs=[whole(n, width), whole(n, width), whole(3, width), whole(3, width), wblk],
         out_specs=[ablk, ablk, whole(n, width), whole(n, width), whole(n, width), whole(n, width), whole(2, width)],
         out_shape=[
             jax.ShapeDtypeStruct((n, hidden), BF16),
@@ -374,23 +374,22 @@
         compiler_params=pltpu.CompilerParams(vmem_limit_bytes=VMEM_LIMIT),
         cost_estimate=pl.CostEstimate(flops=4 * n * width * hidden, bytes_accessed=int(30e6), transcendentals=2 * n * hidden),
         name="ffn",
-    )(r2, ct, gains, shifts, up, down)
-
-
-def ffn_back(dr3, da3, h2b, r2, gains, acts, slopes, up, down):
+    )(r2, ct, gains, shifts, w)
+
+
+def ffn_back(dr3, da3, h2b, r2, gains, acts, slopes, w):
     n, width = r2.shape
-    hidden = up.shape[0]
+    hidden = w.shape[1]
     whole = lambda *s: pl.BlockSpec(s, lambda i: (0,) * len(s))
-    wblk = pl.BlockSpec((FFN_BLOCK, width), lambda i: (i, 0))
+    wblk = pl.BlockSpec((2, FFN_BLOCK, width), lambda i: (0, i, 0))
     ablk = pl.BlockSpec((n, FFN_BLOCK), lambda i: (0, i))
     return pl.pallas_call(
         ffn_back_kernel,
         grid=(hidden // FFN_BLOCK,),
-        in_specs=[whole(n, width), whole(n, width), whole(n, width), whole(n, width), whole(3, width), ablk, ablk, wblk, wblk],
-        out_specs=[wblk, wblk, whole(n, width), whole(n, width), whole(2, width)],
+        in_specs=[whole(n, width), whole(n, width), whole(n, width), whole(n, width), whole(3, width), ablk, ablk, wblk],
+        out_specs=[wblk, whole(n, width), whole(n, width), whole(2, width)],
         out_shape=[
-            jax.ShapeDtypeStruct((hidden, width), BF16),
-            jax.ShapeDtypeStruct((hidden, width), BF16),
+            jax.ShapeDtypeStruct((2, hidden, width), BF16),
             jax.ShapeDtypeStruct((n, width), F32),
             jax.ShapeDtypeStruct((n, width), BF16),
             jax.ShapeDtypeStruct((2, width), F32),
@@ -399,10 +398,10 @@
         compiler_params=pltpu.CompilerParams(vmem_limit_bytes=VMEM_LIMIT),
         cost_estimate=pl.CostEstimate(flops=8 * n * width * hidden, bytes_accessed=int(40e6), transcendentals=0),
         name="ffn_back",
-    )(dr3, da3, h2b, r2, gains, acts, slopes, up, down)
-
-
-def local_step(x, e, ct, t_ids, s_ids, w, gains, shifts):
+    )(dr3, da3, h2b, r2, gains, acts, slopes, w)
+
+
+def local_step(x, e, ct, t_ids, s_ids, w, gains, shifts, halvings):
     x32 = x.astype(F32)
     q, k, v = [dot(x, w["qkv"][c], NT).astype(BF16) for c in range(3)]
     k2, v2 = [dot(e, w["ckv"][c], NT).astype(BF16) for c in range(2)]
@@ -414,11 +413,16 @@
     q2 = dot(h1b, w["cq"], NT).astype(BF16)
     ctx2, lse2 = attend(q2, k2, v2, t_ids, s_ids, fq, fs, False)
     r2 = h1 + dot(ctx2, w["cout"], NN)
-    acts, slopes, layer_out, dr3, da3, h2b, small3 = ffn(r2, ct, gains, shifts, w["up"], w["down"])
-    g_up, g_down, dr2, da2, small2 = ffn_back(dr3, da3, h2b, r2, gains, acts, slopes, w["up"], w["down"])
+    acts, slopes, layer_out, dr3, da3, h2b, small3 = ffn(r2, ct, gains, shifts, w["ffn"])
+    g_ffn, dr2, da2, small2 = ffn_back(dr3, da3, h2b, r2, gains, acts, slopes, w["ffn"])
+    g_ffn = halvings[0](g_ffn)
     g_cout = dot(ctx2, da2, TN).astype(BF16)
     dctx2 = dot(da2, w["cout"], NT).astype(BF16)
+    dctx2, g_ffn = lax.optimization_barrier((dctx2, g_ffn))
+    g_ffn = halvings[1](g_ffn)
     dq2, dk2, dv2 = attend_back(q2, k2, v2, dctx2, ctx2, lse2, t_ids, s_ids, fq, fs, False)
+    dq2, dk2, dv2, g_ffn = lax.optimization_barrier((dq2, dk2, dv2, g_ffn))
+    g_ffn = halvings[2](g_ffn)
     g_cq = dot(dq2, h1b, TN).astype(BF16)
     g_ckv = [dot(dk2, e, TN).astype(BF16), dot(dv2, e, TN).astype(BF16)]
     grad_e = (dot(dk2, w["ckv"][0], NN) + dot(dv2, w["ckv"][1], NN)).astype(BF16)
@@ -428,9 +432,10 @@
     g_out = dot(ctx1, da1, TN).astype(BF16)
     dctx1 = dot(da1, w["out"], NT).astype(BF16)
     dq, dk, dv = attend_back(q, k, v, dctx1, ctx1, lse1, t_ids, t_ids, fq, fk, True)
+    dq, dk, dv, g_ffn = lax.optimization_barrier((dq, dk, dv, g_ffn))
     g_qkv = [dot(d, x, TN).astype(BF16) for d in (dq, dk, dv)]
     grad_x = (dr1 + dot(dq, w["qkv"][0], NN) + dot(dk, w["qkv"][1], NN) + dot(dv, w["qkv"][2], NN)).astype(BF16)
-    grads = dict(qkv=g_qkv, out=g_out, cq=g_cq, ckv=g_ckv, cout=g_cout, up=g_up, down=g_down)
+    grads = dict(qkv=g_qkv, out=g_out, cq=g_cq, ckv=g_ckv, cout=g_cout, ffn=g_ffn)
     grad_gains = jnp.concatenate([gg1, small2[0:1], small3[0:1]], axis=0)
     grad_shifts = jnp.concatenate([gs1, small2[1:2], small3[1:2]], axis=0)
     return layer_out, grad_x, grad_e, grads, grad_gains, grad_shifts
@@ -547,9 +552,9 @@
 
 
 def reduce_kernel(chunks, mats, *refs):
-    grads, small_ref = refs[:mats], refs[mats]
-    (out_ref, small_out_ref, mine, from_c, from_x1, from_y1, from_x2, from_y2, from_z, piece,
-     s_send, s_c, s_x, s_y, s_z, local_sem, send_sem, recv_sem, small_send, small_recv) = refs[mats + 1 :]
+    grads, small_ref, ffn_ref = refs[:mats], refs[mats], refs[mats + 1]
+    (out_ref, small_out_ref, ffn_out_ref, ffn_z, ffn_piece, mine, from_c, from_x1, from_y1, from_x2, from_y2, from_z, piece,
+     s_send, s_c, s_x, s_y, s_z, local_sem, send_sem, recv_sem, small_send, small_recv) = refs[mats + 2 :]
     p, t = lax.axis_index("dp"), lax.axis_index("tensor")
     half = grads[0].shape[1] // 2
     n = half // chunks
@@ -600,6 +605,37 @@
             copy.start()
             local[c].append(copy)
     small = send_small(small_ref, s_c, to_c)
+    f_in = [send(ffn_ref.at[:, zs[j]], ffn_z.at[j], (p, zs[j])) for j in range(3)]
+    f_way = {}
+
+    def ffn_total():
+        for j in range(3):
+            f_in[j].wait_recv()
+        for i in range(2):
+            total = ffn_ref[i, t].astype(F32)
+            for j in range(3):
+                total = total + ffn_z[j, i].astype(F32)
+            ffn_piece[p, i] = total.astype(ffn_piece.dtype)
+        ref = ffn_piece.at[p]
+        f_way["x"] = send(ref, ref, to_x)
+        f_way["y"] = send(ref, ref, to_y)
+        last.append(send(ref, ref, to_c))
+
+    def ffn_far():
+        f_way["x"].wait_recv()
+        ref = ffn_piece.at[to_x[0]]
+        f_way["yd"] = send(ref.at[0], ref.at[0], to_y)
+        last.append(send(ref, ref, to_c))
+        f_way["y"].wait_recv()
+        ref = ffn_piece.at[to_y[0]]
+        f_way["xd"] = send(ref.at[1], ref.at[1], to_x)
+        last.append(send(ref, ref, to_c))
+
+    def ffn_end():
+        f_way["xd"].wait_recv()
+        f_way["yd"].wait_recv()
+        ref = ffn_piece.at[jnp.bitwise_xor(p, 6)]
+        last.append(send(ref, ref, to_c))
 
     def add(dst, src):
         dst[...] = (dst[...].astype(F32) + src[...].astype(F32)).astype(dst.dtype)
@@ -687,6 +723,11 @@
             s_send[2] = s_send[1] + s_y[...]
             s_z[t] = s_send[2]
             small = [send_small(s_send.at[2], s_z.at[t], (p, z)) for z in zs]
+            ffn_total()
+        elif step == 4:
+            ffn_far()
+        elif step == 5:
+            ffn_end()
     for copy in small:
         copy.wait()
     small_out_ref[...] = (s_z[0] + s_z[1]) + (s_z[2] + s_z[3])
@@ -696,22 +737,33 @@
         copy.wait_send()
     for a in range(mats):
         out_ref[a] = piece[a].astype(out_ref.dtype)
-
-
-def reduce_pack(grads, small, collective_id, chunks=3):
+    part = ffn_piece.shape[2]
+    for a in range(8):
+        for i in range(2):
+            ffn_out_ref[i, pl.ds(a * part, part), :] = ffn_piece[a, i].astype(ffn_out_ref.dtype)
+
+
+def reduce_pack(grads, small, ffn, collective_id, chunks=3):
     mats = len(grads)
     tensor, rows, width = grads[0].shape
     half, per = rows // 2, mats // 4
-    count = chunks * (mats + 4 + 2 + 3 + 3 + 4 + 1)
+    part = ffn.shape[2]
+    count = chunks * (mats + 4 + 2 + 3 + 3 + 4 + 1) + 11
     vmem = pl.BlockSpec(memory_space=pltpu.VMEM)
     buf = lambda *s: pltpu.VMEM(s + (half, width), BF16)
     sb = lambda *s: pltpu.VMEM(s + small.shape, F32)
     return pl.pallas_call(
         functools.partial(reduce_kernel, chunks, mats),
-        out_shape=(jax.ShapeDtypeStruct((mats, rows, width), F32), jax.ShapeDtypeStruct(small.shape, F32)),
-        in_specs=[pl.BlockSpec(memory_space=pl.ANY)] * mats + [vmem],
-        out_specs=(vmem, vmem),
+        out_shape=(
+            jax.ShapeDtypeStruct((mats, rows, width), F32),
+            jax.ShapeDtypeStruct(small.shape, F32),
+            jax.ShapeDtypeStruct((2, 8 * part, width), F32),
+        ),
+        in_specs=[pl.BlockSpec(memory_space=pl.ANY)] * mats + [vmem, vmem],
+        out_specs=(vmem, vmem, vmem),
         scratch_shapes=[
+            pltpu.VMEM((3, 2, part, width), BF16),
+            pltpu.VMEM((8, 2, part, width), BF16),
             buf(mats, 4), buf(mats, 4), buf(2, per, 2), buf(2, per, 2), buf(per, 2), buf(per, 2), buf(3, per),
             pltpu.VMEM((mats, rows, width), BF16),
             sb(3), sb(), sb(), sb(), sb(4),
@@ -726,13 +778,45 @@
         ),
         cost_estimate=pl.CostEstimate(flops=int(1e9), bytes_accessed=int(60e6), transcendentals=0),
         name="reduce_pack",
-    )(*grads, small)
+    )(*grads, small, ffn)
+
+
+def flip(x, bit):
+    return lax.ppermute(x, "dp", [(i, i ^ bit) for i in range(lax.axis_size("dp"))])
+
+
+def take(x, i, axis):
+    return lax.dynamic_index_in_dim(x, i, axis, keepdims=False)
+
+
+def halve_core(grad):
+    tensor = lax.axis_size("tensor")
+    core = lax.axis_index("dp") % 2
+    grad = grad.reshape(2, 2, 2, 2, tensor, grad.shape[1] // (8 * tensor), grad.shape[2])
+    return take(grad, core, 3) + flip(take(grad, 1 - core, 3), 1)
+
+
+def halve_plane(grad):
+    p = lax.axis_index("dp")
+    cx, cy = p // 2 % 2, p // 4
+    cut = grad.shape[3] // 2
+    left, right = grad[:, :, :, :cut], grad[:, :, :, cut:]
+    left_in, right_in = flip(take(left, 1 - cx, 2), 2), flip(take(right, 1 - cy, 1), 4)
+    return take(left, cx, 2) + left_in, take(right, cy, 1) + right_in
+
+
+def halve_rest(halves):
+    left, right = halves
+    p = lax.axis_index("dp")
+    cx, cy = p // 2 % 2, p // 4
+    left_in, right_in = flip(take(left, 1 - cy, 1), 4), flip(take(right, 1 - cx, 1), 2)
+    return jnp.concatenate([take(left, cy, 1) + left_in, take(right, cx, 1) + right_in], axis=1)
 
 
 def gather_rows(shard):
     mats, rows, width = shard.shape
     dp, tensor = lax.axis_size("dp"), lax.axis_size("tensor")
-    if (dp, tensor, mats) == (8, 4, 8):
+    if own_kernels():
         return gather_pack(shard, 0).reshape(mats, tensor * rows, width)
     piece = mats * rows // dp
     mine = lax.dynamic_slice_in_dim(
@@ -743,20 +827,26 @@
     return full.reshape(mats, tensor * rows, width)
 
 
-def reduce_rows(grads, small):
+def own_kernels():
+    return (lax.axis_size("dp"), lax.axis_size("tensor")) == (8, 4)
+
+
+def reduce_rows(grads, small, ffn):
     mats = len(grads)
     all_rows, width = grads[0].shape
     dp, tensor = lax.axis_size("dp"), lax.axis_size("tensor")
     rows = all_rows // tensor
-    if (dp, tensor, mats) == (8, 4, 8):
-        return reduce_pack([g.reshape(tensor, rows, width) for g in grads], small, 1)
+    if own_kernels():
+        return reduce_pack([g.reshape(tensor, rows, width) for g in grads], small, ffn, 1)
     piece = mats * rows // dp
     grad = jnp.stack(grads).reshape(mats, tensor, dp // mats, piece, width).transpose(0, 2, 1, 3, 4)
     mine = lax.psum_scatter(
         grad.reshape(dp * tensor * piece, width), ("dp", "tensor"), scatter_dimension=0, tiled=True
     )
     total = lax.all_gather(mine, "dp", axis=0, tiled=True).reshape(mats, rows, width).astype(F32)
-    return total, lax.psum(small, ("dp", "tensor"))
+    ffn = lax.psum_scatter(ffn, ("dp", "tensor"), scatter_dimension=1, tiled=True)
+    ffn = lax.all_gather(ffn, "dp", axis=1, tiled=True).astype(F32)
+    return total, lax.psum(small, ("dp", "tensor")), ffn
 
 
 def per_device(
@@ -781,23 +871,17 @@
     dp, tensor = lax.axis_size("dp"), lax.axis_size("tensor")
     piece = hidden // dp
     start = lax.axis_index("dp") * piece
-    up, down = [
-        lax.all_gather(lax.dynamic_slice_in_dim(m, start, piece, 0), ("dp", "tensor"), axis=0, tiled=True)
-        for m in (ffn_up.T, ffn_down)
-    ]
-    w = dict(qkv=pack[0:3], out=pack[3], cq=pack[4], ckv=pack[5:7], cout=pack[7], up=up, down=down)
+    ffn_w = jnp.stack([ffn_up.T, ffn_down], axis=0)
+    ffn_w = lax.dynamic_slice_in_dim(ffn_w, start, piece, 1)
+    ffn_w = lax.all_gather(ffn_w, ("dp", "tensor"), axis=1, tiled=True)
+    w = dict(qkv=pack[0:3], out=pack[3], cq=pack[4], ckv=pack[5:7], cout=pack[7], ffn=ffn_w)
+    halvings = (halve_core, halve_plane, halve_rest) if own_kernels() else (lambda g: g,) * 3
     layer_out, grad_x, grad_e, grads, grad_gains, grad_shifts = local_step(
-        inputs, encoded, cotangent, t_ids, s_ids, w, gains, shifts
+        inputs, encoded, cotangent, t_ids, s_ids, w, gains, shifts, halvings
     )
-    g_up, g_down = [
-        lax.all_gather(
-            lax.psum_scatter(grads[name], ("dp", "tensor"), scatter_dimension=0, tiled=True), "dp", axis=0, tiled=True
-        )
-        for name in ("up", "down")
-    ]
     small = jnp.concatenate([grad_gains, grad_shifts, jnp.zeros((2, width), F32)], axis=0)
-    total, small = reduce_rows(
-        [*grads["qkv"], grads["out"], grads["cq"], *grads["ckv"], grads["cout"]], small
+    total, small, g_ffn = reduce_rows(
+        [*grads["qkv"], grads["out"], grads["cq"], *grads["ckv"], grads["cout"]], small, grads["ffn"]
     )
     return (
         layer_out,
@@ -808,8 +892,8 @@
         total[4].T,
         total[5:7].transpose(0, 2, 1),
         total[7],
-        g_up.astype(F32).T,
-        g_down.astype(F32),
+        g_ffn[0].T,
+        g_ffn[1],
         small[0:3],
         small[3:6],
     )

time: 502 us -> 468 us (0.932)
  waiting for transfers between devices: 87.1 us -> 0.08 us
  Pallas kernels: 279 us -> 306 us
  local copies, waits for them, and re-layouts: 24.9 us -> 41.2 us
  starting transfers between devices: 0.42 us -> 9.04 us
  other arithmetic: 12.2 us -> 19.9 us
    all_gather x4 -> x1, waiting for transfers between devices: 52.5 us -> 0.01 us  [per_device(): ffn_w = lax.all_gather(ffn_w, ('dp', 'tensor'), axis=1, tiled=True)]
    reduce_scatter x2 -> x0, waiting for transfers between devices: 34.5 us -> none  [per_device(): lax.psum_scatter(grads[name], ('dp', 'tensor'), scatter_dimension=0, tile...]
    pallas_call x1, Pallas kernels: 78 us -> 91.9 us  [reduce_pack(): pl.pallas_call(functools.partial(reduce_kernel, chunks, mats), out_shape=...]
    squeeze x0 -> x6, local copies, waits for them, and re-layouts: none -> 9.43 us  [the longest x5 6.91 us: take(): return lax.dynamic_index_in_dim(x, i, axis, keepdims=False)]
    ppermute x0 -> x5, starting transfers between devices: none -> 9 us  [flip(): lax.ppermute(x, 'dp', [(i, i ^ bit) for i in range(lax.axis_size('dp'))])]
    add x0 -> x5, other arithmetic: none -> 8.81 us  [the longest x2 3.37 us: halve_plane(): return (take(left, cx, 2) + left_in, take(right, cy, 1) + right_in)]
    pallas_call x1, Pallas kernels: 50.6 us -> 57.4 us  [gather_pack(): pl.pallas_call(functools.partial(gather_kernel, groups, chunks, window),...]
    unnamed x98 -> x104, local copies, waits for them, and re-layouts: 7.14 us -> 13.2 us
  transfers between devices with their start and end apart: 6 -> 6, of which waited for: 5 -> 1; matrix products, arithmetic and copies ran while one was open for 21% -> 14% of each run, Pallas kernels for 45% -> 34%
where the time goes in v1:
time: 468 us; the launch traced here: 462 us
  Pallas kernels  306 us (65%)
  matrix products  70.5 us (15%)
  local copies, waits for them, and re-layouts  41.2 us (9%)
  other arithmetic  19.9 us (4%)
  between operations  14.9 us (3%)
  starting transfers between devices  9.04 us (2%)
    pallas_call x1, Pallas kernels, reduce_pack(): pl.pallas_call(functools.partial(reduce_kernel, chunks, mats), out_shape=...  91.9 us
    dot_general x24, matrix products, dot(): return lax.dot_general(a, b, dims, preferred_element_type=F32)  70.5 us
    pallas_call x2, Pallas kernels, attend_back(): pl.pallas_call(functools.partial(attend_back_kernel, causal, block, per),...  57.8 us
    pallas_call x1, Pallas kernels, gather_pack(): pl.pallas_call(functools.partial(gather_kernel, groups, chunks, window),...  57.4 us
    pallas_call x2, Pallas kernels, attend(): pl.pallas_call(functools.partial(attend_kernel, causal, block, per), out_...  40.3 us
    pallas_call x1, Pallas kernels, ffn_back(): pl.pallas_call(ffn_back_kernel, grid=(hidden // FFN_BLOCK,), in_specs=[wh...  33 us
    pallas_call x1, Pallas kernels, ffn(): pl.pallas_call(ffn_kernel, grid=(hidden // FFN_BLOCK,), in_specs=[whole(n...  25.8 us
    unnamed x104, local copies, waits for them, and re-layouts  13.2 us
  transfers between devices with their start and end apart: 6, of which 1 were waited for; matrix products, arithmetic and copies ran while one was open for 14% of the time, Pallas kernels for 34%

profile of v1, /device:TPU:0, one launch (start us, length us, event | category | flops | bytes accessed | tf_op | source)
XLA Modules:
  0.0 461.7 jit_solution(9861243083318158010)
XLA Ops:
  16.2 57.4 %gather_pack.1 = bf16[8,4,192,768]{3,2,1,0:T(8,128)(2,1)S(1)} custom-call(bf16[8,192,768]{2,1,0:T(8,128)(2,1)S(1)} %bitcast_dynamic-update-slice_fusion.3.pack_ref), custom_call_target="tpu_custom_call" | custom-call | tf_op jit(solution)/shard_map/gather_pack/pallas_call | solution.py:539
  73.6 3.6 copy-done.1
  82.4 5.4 %fusion.17 = (bf16[1,4,192,768]{3,2,1,0:T(8,128)(2,1)}, bf16[1,4,192,768]{3,2,1,0:T(8,128)(2,1)S(1)}, bf16[1,4,192,768]{3,2,1,0:T(8,128)(2,1)S(1)}, bf16[1,4,192...) fusion(bf16[8,4,192,768]{3,2,1,0:T(8,128)(2,1)} %copy-done.1), kind=kLoop, calls=%fused_computation.114 | loop fusion | bytes 18874368 | tf_op jit(solution)/shard_map/slice | solution.py:877
  87.9 3.1 fusion.2.q_ref
  96.1 17.6 %attend.2 = (bf16[1024,768]{1,0:T(8,128)(2,1)}, f32[6,4,1,512]{3,2,1,0:T(1,128)}) custom-call(s32[4]{0:T(128)} %and_select_fusion.5.lo_ref, s32[4]{0:T(128)} %and_select_fusion.4.hi_ref, bf16[1024,768]{1,0:T(8,128)(2,1)} %fusion.2.q_ref, bf16[1024,768]{1,0:T(8,128)(2,1)} %fusion.3.k_ref, bf16[1024,768]{1,0:T(8,128)(2,1)} %fusion.4.v_ref, ...), custom_call_target="tpu_custom_call" | custom-call | flops 8000000000 | bytes 8000000 | tf_op jit(solution)/shard_map/attend/pallas_call | solution.py:188
  113.7 3.4 fusion.22
  126.8 22.7 %attend.3 = (bf16[1024,768]{1,0:T(8,128)(2,1)}, f32[6,4,1,512]{3,2,1,0:T(1,128)}) custom-call(s32[4]{0:T(128)} %and_select_fusion.3.lo_ref, s32[4]{0:T(128)} %and_select_fusion.2.hi_ref, bf16[1024,768]{1,0:T(8,128)(2,1)} %convolution_convert_fusion.4.q_ref, bf16[1024,768]{1,0:T(8,128)(2,1)} %fusion.5.k_ref, bf16[1024,768]{1,0:T(8,128)(2,1)} %fusion.6.v_ref, ...), custom_call_target="tpu_custom_call" | custom-call | flops 8000000000 | bytes 8000000 | tf_op jit(solution)/shard_map/attend/pallas_call | solution.py:188
  149.4 4.5 fusion.r2_ref
  153.9 25.8 %ffn.1 = (bf16[1024,3072]{1,0:T(8,128)(2,1)}, bf16[1024,3072]{1,0:T(8,128)(2,1)}, bf16[1024,768]{1,0:T(8,128)(2,1)}, f32[1024,768]{1,0:T(8,128)}, bf16[1024,768]...) custom-call(f32[1024,768]{1,0:T(8,128)} %fusion.r2_ref, bf16[1024,768]{1,0:T(8,128)(2,1)} %ct_ref.1, ...), custom_call_target="tpu_custom_call" | custom-call | flops 9663676416 | bytes 30000000 | tf_op jit(solution)/shard_map/ffn/pallas_call | solution.py:359
  179.8 33.0 %ffn_back.1 = (bf16[2,3072,768]{2,1,0:T(8,128)(2,1)}, f32[1024,768]{1,0:T(8,128)}, bf16[1024,768]{1,0:T(8,128)(2,1)}, f32[2,768]{1,0:T(2,128)}) custom-call(f32[1024,768]{1,0:T(8,128)} %get-tuple-element.50.dr3_ref, bf16[1024,768]{1,0:T(8,128)(2,1)} %get-tuple-element.51.da3_ref, bf16[1024,768]{1,0:T(8,128)(2,1)} %get-tuple-element.52.h2b_ref, ...), custom_call_target="tpu_custom_call" | custom-call | flops 19327352832 | bytes 40000000 | tf_op jit(solution)/shard_map/ffn_back/pallas_call | solution.py:386
  212.8 4.8 %dynamic-slice_bitcast_fusion = bf16[2,2,2,4,96,768]{5,4,3,2,1,0:T(8,128)(2,1)} fusion(bf16[2,2,2,2,4,96,768]{6,5,4,3,2,1,0:T(8,128)(2,1)} %bitcast.136, s32[]{:T(128)S(6)} %select_n.93), kind=kLoop, calls=%fused_computation.1 | loop fusion | bytes 9437188 | tf_op jit(solution)/shard_map/jit(dynamic_index_in_dim)/squeeze | solution.py:789
  219.2 4.1 convolution_convert_fusion.1.g_ref
  225.9 2.9 bitcast_add_fusion
  233.0 3.3 collective-permute-start.1
  236.4 31.8 %attend_back.2 = (bf16[1024,768]{1,0:T(8,128)(2,1)}, bf16[1024,768]{1,0:T(8,128)(2,1)}, bf16[1024,768]{1,0:T(8,128)(2,1)}) custom-call(s32[4]{0:T(128)} %and_select_fusion.1.lo_ref, s32[4]{0:T(128)} %and_select_fusion.hi_ref, bf16[1024,768]{1,0:T(8,128)(2,1)} %convolution_convert_fusion.4.q_ref, bf16[1024,768]{1,0:T(8,128)(2,1)} %fusion.5.k_ref, ...), custom_call_target="tpu_custom_call" | custom-call | flops 20000000000 | bytes 12000000 | tf_op jit(solution)/shard_map/attend_back/pallas_call | solution.py:217
  287.1 3.0 fusion.25
  290.2 26.0 %attend_back.3 = (bf16[1024,768]{1,0:T(8,128)(2,1)}, bf16[1024,768]{1,0:T(8,128)(2,1)}, bf16[1024,768]{1,0:T(8,128)(2,1)}) custom-call(s32[4]{0:T(128)} %and_select_fusion.5.lo_ref, s32[4]{0:T(128)} %and_select_fusion.4.hi_ref, bf16[1024,768]{1,0:T(8,128)(2,1)} %fusion.2.q_ref, bf16[1024,768]{1,0:T(8,128)(2,1)} %fusion.3.k_ref, ...), custom_call_target="tpu_custom_call" | custom-call | flops 20000000000 | bytes 12000000 | tf_op jit(solution)/shard_map/attend_back/pallas_call | solution.py:217
  316.2 3.9 add_convert_fusion
  320.2 4.0 convolution_convert_fusion.10
  335.7 91.9 %reduce_pack.1 = (f32[8,192,768]{2,1,0:T(8,128)}, f32[8,768]{1,0:T(8,128)S(1)}, f32[2,768,768]{2,1,0:T(8,128)}) custom-call(bf16[4,192,768]{2,1,0:T(8,128)(2,1)S(1)} %bitcast.133, bf16[4,192,768]{2,1,0:T(8,128)(2,1)S(1)} %bitcast.134, bf16[4,192,768]{2,1,0:T(8,128)(2,1)S(1)} %bitcast.135, bf16[4,192,768]{2,1,0:T(8,128)(2,1)S(1)} %bitcast.132, ...), custom_call_target="tpu_custom_call" | custom-call | flops 1000000000 | bytes 60000000 | tf_op jit(solution)/shard_map/reduce_pack/pallas_call | solution.py:755
  435.5 3.0 fusion.23
  438.5 3.0 fusion.24
  444.1 3.1 copy.63
  447.9 6.8 %add_convert_fusion.1 = bf16[1024,768]{1,0:T(8,128)(2,1)} fusion(f32[1024,768]{1,0:T(8,128)} %fusion.24, f32[1024,768]{1,0:T(8,128)} %copy-done.5, f32[1024,768]{1,0:T(8,128)} %fusion.23, bf16[1024,768]{1,0:T(8,128)(2,1)} %get-tuple-element.73, bf16[768,768]{1,0:T(8,128)(2,1)S(1)} %bitcast.141), kind=kOutput, calls=%fused_computation.4 | convolution fusion | flops 1211105280 | bytes 13762560 | tf_op jit(solution)/shard_map/dot_general | solution.py:20
  (177 shorter events, 78.5 us)
Async XLA Ops:
  7.2 111.7 %copy-start = (bf16[1024,768]{1,0:T(8,128)(2,1)S(1)}, bf16[1024,768]{1,0:T(8,128)(2,1)}, u32[]{:S(2)}) copy-start(bf16[1024,768]{1,0:T(8,128)(2,1)} %param.15) | copy-start | bytes 4718596
  7.2 146.7 %all-gather.2.cloned.1.call-start = ((), (), s32[]{:S(2)}) async-start(), calls=%async_computation | async-start | bytes 9732096 | tf_op jit(solution)/shard_map/all_gather | solution.py:876
  82.4 5.4 %copy-start.32 = (bf16[1024,768]{1,0:T(8,128)(2,1)S(1)}, bf16[1024,768]{1,0:T(8,128)(2,1)}, u32[]{:S(2)}) copy-start(bf16[1024,768]{1,0:T(8,128)(2,1)} %param.14) | copy-start | bytes 4718596
  87.8 5.7 %copy-start.6 = (bf16[1,4,192,768]{3,2,1,0:T(8,128)(2,1)}, bf16[1,4,192,768]{3,2,1,0:T(8,128)(2,1)S(1)}, u32[]{:S(2)}) copy-start(bf16[1,4,192,768]{3,2,1,0:T(8,128)(2,1)S(1)} %get-tuple-element.155) | copy-start | bytes 3538948
  87.8 25.9 %copy-start.21 = (bf16[1,4,192,768]{3,2,1,0:T(8,128)(2,1)}, bf16[1,4,192,768]{3,2,1,0:T(8,128)(2,1)S(1)}, u32[]{:S(2)}) copy-start(bf16[1,4,192,768]{3,2,1,0:T(8,128)(2,1)S(1)} %get-tuple-element.154) | copy-start | bytes 3538948
  87.8 31.0 %copy-start.17 = (bf16[1,4,192,768]{3,2,1,0:T(8,128)(2,1)}, bf16[1,4,192,768]{3,2,1,0:T(8,128)(2,1)S(1)}, u32[]{:S(2)}) copy-start(bf16[1,4,192,768]{3,2,1,0:T(8,128)(2,1)S(1)} %get-tuple-element.152) | copy-start | bytes 3538948
  87.8 33.6 %copy-start.19 = (bf16[1,4,192,768]{3,2,1,0:T(8,128)(2,1)}, bf16[1,4,192,768]{3,2,1,0:T(8,128)(2,1)S(1)}, u32[]{:S(2)}) copy-start(bf16[1,4,192,768]{3,2,1,0:T(8,128)(2,1)S(1)} %get-tuple-element.151) | copy-start | bytes 3538948
  117.1 32.3 %copy-start.3 = (f32[1024,768]{1,0:T(8,128)}, f32[1024,768]{1,0:T(8,128)S(1)}, u32[]{:S(2)}) copy-start(f32[1024,768]{1,0:T(8,128)S(1)} %get-tuple-element.172) | copy-start | bytes 9437188
  126.8 22.7 %copy-start.25 = (bf16[1,4,192,768]{3,2,1,0:T(8,128)(2,1)S(1)}, bf16[1,4,192,768]{3,2,1,0:T(8,128)(2,1)}, u32[]{:S(2)}) copy-start(bf16[1,4,192,768]{3,2,1,0:T(8,128)(2,1)} %get-tuple-element.150) | copy-start | bytes 3538948
  212.8 6.4 %copy-start.31 = (f32[2,768]{1,0:T(2,128)S(1)}, f32[2,768]{1,0:T(2,128)}, u32[]{:S(2)}) copy-start(f32[2,768]{1,0:T(2,128)} %get-tuple-element.76) | copy-start | bytes 18436
  212.8 6.4 %copy-start.30 = (f32[2,768]{1,0:T(2,128)S(1)}, f32[2,768]{1,0:T(2,128)}, u32[]{:S(2)}) copy-start(f32[2,768]{1,0:T(2,128)} %get-tuple-element.77) | copy-start | bytes 18436
  217.6 8.3 %collective-permute-start = (bf16[2,2,2,4,96,768]{5,4,3,2,1,0:T(8,128)(2,1)}, bf16[2,2,2,4,96,768]{5,4,3,2,1,0:T(8,128)(2,1)}, u32[]{:S(2)}, u32[]{:S(2)}) collective-permute-start(bf16[2,2,2,4,96,768]{5,4,3,2,1,0:T(8,128)(2,1)} %dynamic-slice_bitcast_fusion), channel_id=1, source_target_pairs={{0,4},{4,0},{8,12},{12,8},{16,20},{20,16},{24,28},{28,24},{1,5},{5... | collective-permute-start | bytes 14155784 | tf_op jit(solution)/shard_map/ppermute | solution.py:785
  219.2 6.7 %slice-start = ((s8[9437184]{0:T(1024)(128)(4,1)}), s8[4194304]{0:T(1024)(128)(4,1)S(1)}, s32[]{:S(2)}) async-start(s8[9437184]{0:T(1024)(128)(4,1)} %bitcast.137), calls=%async_computation.1 | async-start | bytes 8388608
  219.2 6.7 %slice-start.1 = ((s8[9437184]{0:T(1024)(128)(4,1)}), s8[4194304]{0:T(1024)(128)(4,1)S(1)}, s32[]{:S(2)}) async-start(s8[9437184]{0:T(1024)(128)(4,1)} %bitcast.137), calls=%async_computation.2 | async-start | bytes 8388608
  230.3 37.9 %collective-permute-start.2 = (bf16[2,2,2,96,768]{4,3,2,1,0:T(8,128)(2,1)}, bf16[2,2,2,96,768]{4,3,2,1,0:T(8,128)(2,1)}, u32[]{:S(2)}, u32[]{:S(2)}) collective-permute-start(bf16[2,2,2,96,768]{4,3,2,1,0:T(8,128)(2,1)} %dynamic-slice_bitcast_fusion.1), channel_id=1, source_target_pairs={{0,16},{4,20},{8,24},{12,28},{16,0},{20,4},{24,8},{28,12},{1,17},{... | collective-permute-start | bytes 3538952 | tf_op jit(solution)/shard_map/ppermute | solution.py:785
  233.0 36.7 %collective-permute-start.1 = (bf16[2,2,2,96,768]{4,3,2,1,0:T(8,128)(2,1)S(1)}, bf16[2,2,2,96,768]{4,3,2,1,0:T(8,128)(2,1)}, u32[]{:S(2)}, u32[]{:S(2)}) collective-permute-start(bf16[2,2,2,96,768]{4,3,2,1,0:T(8,128)(2,1)S(1)} %dynamic-slice_bitcast_fusion.2), channel_id=1, source_target_pairs={{0,8},{4,12},{8,0},{12,4},{16,24},{20,28},{24,16},{28,20},{1,9},{5... | collective-permute-start | bytes 3538952 | tf_op jit(solution)/shard_map/ppermute | solution.py:785
  269.7 14.8 %copy-start.8 = (bf16[2,2,2,96,768]{4,3,2,1,0:T(8,128)(2,1)}, bf16[2,2,2,96,768]{4,3,2,1,0:T(8,128)(2,1)S(1)}, u32[]{:S(2)}) copy-start(bf16[2,2,2,96,768]{4,3,2,1,0:T(8,128)(2,1)S(1)} %bitcast_add_fusion.1) | copy-start | bytes 3538948
  271.6 12.0 %copy-start.10 = (bf16[2,2,2,96,768]{4,3,2,1,0:T(8,128)(2,1)}, bf16[2,2,2,96,768]{4,3,2,1,0:T(8,128)(2,1)S(1)}, u32[]{:S(2)}) copy-start(bf16[2,2,2,96,768]{4,3,2,1,0:T(8,128)(2,1)S(1)} %bitcast_add_fusion.2) | copy-start | bytes 3538948
  281.0 6.1 %copy-start.37 = (bf16[1024,768]{1,0:T(8,128)(2,1)S(1)}, bf16[1024,768]{1,0:T(8,128)(2,1)}, u32[]{:S(2)}) copy-start(bf16[1024,768]{1,0:T(8,128)(2,1)} %get-tuple-element.75) | copy-start | bytes 4718596
  284.5 42.2 %collective-permute-start.3 = (bf16[2,2,96,768]{3,2,1,0:T(8,128)(2,1)}, bf16[2,2,96,768]{3,2,1,0:T(8,128)(2,1)}, u32[]{:S(2)}, u32[]{:S(2)}) collective-permute-start(bf16[2,2,96,768]{3,2,1,0:T(8,128)(2,1)} %dynamic-slice_bitcast_fusion.4), channel_id=1, source_target_pairs={{0,16},{4,20},{8,24},{12,28},{16,0},{20,4},{24,8},{28,12},{1,17},{... | collective-permute-start | bytes 1769480 | tf_op jit(solution)/shard_map/ppermute | solution.py:785
  284.5 43.4 %collective-permute-start.4 = (bf16[2,2,96,768]{3,2,1,0:T(8,128)(2,1)S(1)}, bf16[2,2,96,768]{3,2,1,0:T(8,128)(2,1)}, u32[]{:S(2)}, u32[]{:S(2)}) collective-permute-start(bf16[2,2,96,768]{3,2,1,0:T(8,128)(2,1)S(1)} %dynamic-slice_bitcast_fusion.3), channel_id=1, source_target_pairs={{0,8},{4,12},{8,0},{12,4},{16,24},{20,28},{24,16},{28,20},{1,9},{5... | collective-permute-start | bytes 1769480 | tf_op jit(solution)/shard_map/ppermute | solution.py:785
  290.2 26.1 %copy-start.18 = (bf16[1,4,192,768]{3,2,1,0:T(8,128)(2,1)S(1)}, bf16[1,4,192,768]{3,2,1,0:T(8,128)(2,1)}, u32[]{:S(2)}) copy-start(bf16[1,4,192,768]{3,2,1,0:T(8,128)(2,1)} %copy-done.17) | copy-start | bytes 3538948
  290.2 26.1 %copy-start.36 = (f32[1024,768]{1,0:T(8,128)S(1)}, f32[1024,768]{1,0:T(8,128)}, u32[]{:S(2)}) copy-start(f32[1024,768]{1,0:T(8,128)} %fusion.25) | copy-start | bytes 9437188
  435.5 6.1 %slice-start.3 = ((s8[4718592]{0:T(1024)(128)(4,1)}), s8[4194304]{0:T(1024)(128)(4,1)S(1)}, s32[]{:S(2)}) async-start(s8[4718592]{0:T(1024)(128)(4,1)} %bitcast.142), calls=%async_computation.4 | async-start | bytes 8388608
  (31 other events, 87.3 us)
Sparse Core Ops, SparseCore 0:
  11.7 100.5 all-gather.1
